TPU v7x, 128 devices: a whole 4x4x4 slice. The times are simulated.
128 devices in a mesh: sect: 8 (over z, core), blk: 16 (over x, y).
Axes of the slice: x: 4, y: 4, z: 4, core: 2. Of those that a mesh axis runs over, the one named last changes fastest.
Arguments:
- left_boundary: bfloat16 [8, 17, 64, 128, 128], P('sect', None, 'blk'), may hold values from -4 to 4, as said below
- right_boundary: bfloat16 [8, 17, 64, 128, 128], P('sect', None, 'blk'), may hold values from -4 to 4, as said below
- psi_start: float32 [8, 384, 128, 128], P('sect', 'blk'), may hold values from -6 to 6
- left_local: int32 [8, 384], P('sect'), may hold values from 0 to 3
- right_group: int32 [8, 384, 1], P('sect'), may hold values from 0 to 15; in each aligned block of 24 rows (0 to 23, 24 to 47, ..., all dimensions but the last counted through in order) at most 2 rows name the same one
- right_local: int32 [8, 384], P('sect'), may hold values from 0 to 3
- left_dims: int32 [8, 64], P('sect'), may hold values from 64 to 128
- right_dims: int32 [8, 64], P('sect'), may hold values from 64 to 128
- left_mix: float32 [17, 17], replicated, may hold values from -1.5 to 1.5
- right_mix: float32 [17, 17], replicated, may hold values from -1.5 to 1.5
Outputs:
- wave: bfloat16 [8, 384, 128, 128], P('sect', 'blk')
- energy: float32 [8], P('sect')
- left_grown: bfloat16 [8, 17, 64, 128, 128], P('sect', None, 'blk')
- right_grown: bfloat16 [8, 17, 64, 128, 128], P('sect', None, 'blk')
Inputs may be any that keep to these rules, and one draw needn't show every extreme that they name: `right_group`: among the blocks e of each aligned run of 24 blocks of a section, at most 2 share one value, and some run reaches 2. `left_boundary`: every block of every channel and sector is symmetric. `right_boundary`: every block of every channel and sector is symmetric.
All inputs are finite; a program needn't handle non-finite values.
Results may differ from a plain program's by a relative error of at most 0.012.
Values may be sent and summed in bfloat16 or wider, within the bound.
A program may use at most 256 MiB of HBM per device.

v0:
```python
import math

import jax
import jax.numpy as jnp
from jax import lax
from jax.sharding import PartitionSpec as P

ITERS = 2


EPSILON = 1e-06


def from_behind(block, axis, distance):
    devices = range(lax.axis_size(axis))
    route = [(i - distance, i) for i in devices if i - distance in devices]
    return lax.ppermute(block, axis, route)


def vacuum_blocks(channels, sectors_dev, block_size, channel):
    rows = jnp.arange(block_size)[:, None]
    cols = jnp.arange(block_size)[None, :]
    eye = jnp.where(rows == cols, 1.0, 0.0).astype(jnp.float32)
    chan = (jnp.arange(channels) == channel).astype(jnp.float32)
    blocks = (
        chan[:, None, None, None]
        * eye[None, None, :, :]
        * jnp.ones((1, sectors_dev, 1, 1), jnp.float32)
    )
    return blocks.astype(jnp.bfloat16)


def body(
    left_boundary,
    right_boundary,
    psi_start,
    left_local,
    right_group,
    right_local,
    left_dims,
    right_dims,
    left_mix,
    right_mix,
):
    hi = lax.Precision.HIGHEST
    channels = left_boundary.shape[1]
    sectors_dev = left_boundary.shape[2]
    block_size = left_boundary.shape[3]
    entries = psi_start.shape[1]
    n_blocks = lax.axis_size("blk")
    slot_count = max(2, entries // n_blocks + 1)
    my_index = lax.axis_index("blk")
    section = lax.axis_index("sect")
    last_section = lax.axis_size("sect") - 1
    inv_root = 1.0 / math.sqrt(block_size)
    left_env = from_behind(left_boundary, "sect", 1)[0]
    right_env = from_behind(right_boundary, "sect", -1)[0]
    left_env = jnp.where(
        section == 0, vacuum_blocks(channels, sectors_dev, block_size, 0), left_env
    )
    right_env = jnp.where(
        section == last_section,
        vacuum_blocks(channels, sectors_dev, block_size, channels - 1),
        right_env,
    )
    groups = right_group[0, :, 0].reshape(n_blocks, entries)
    right_loc = right_local[0].reshape(n_blocks, entries)
    left_mine = lax.dynamic_slice_in_dim(left_local[0], my_index * entries, entries)
    positions = jnp.arange(entries)
    earlier = positions[None, :] < positions[:, None]
    same_group = groups[:, :, None] == groups[:, None, :]
    ranks = jnp.sum(jnp.logical_and(same_group, earlier[None, :, :]), axis=2)
    group_mine = jnp.take(groups, my_index, axis=0)
    rank_mine = jnp.take(ranks, my_index, axis=0)
    right_mine = jnp.take(right_loc, my_index, axis=0)
    slot_mine = group_mine * slot_count + rank_mine
    owned = groups == my_index
    picks = jnp.logical_and(
        owned[:, None, :], ranks[:, None, :] == jnp.arange(slot_count)[None, :, None]
    )
    slot_sector = jnp.sum(jnp.where(picks, right_loc[:, None, :], 0), axis=2).reshape(-1)
    slot_live = jnp.any(picks, axis=2).reshape(-1)
    left_global = my_index * sectors_dev + left_mine
    right_global = group_mine * sectors_dev + right_mine
    row_live = jnp.arange(block_size)[None, :] < jnp.take(left_dims[0], left_global)[:, None]
    col_live = jnp.arange(block_size)[None, :] < jnp.take(right_dims[0], right_global)[:, None]
    mask = jnp.logical_and(row_live[:, :, None], col_live[:, None, :]).astype(jnp.float32)
    left_sel = jnp.take(left_env, left_mine, axis=1)
    outgoing = jnp.take(right_env, slot_sector, axis=1)
    incoming = lax.all_to_all(outgoing, "blk", split_axis=1, concat_axis=1, tiled=True)
    right_sel = jnp.take(incoming, slot_mine, axis=1)

    def hamiltonian(vector):
        rounded = vector.astype(jnp.bfloat16)
        inner = jnp.einsum(
            "kexa,eab->kexb", left_sel, rounded, preferred_element_type=jnp.float32
        ).astype(jnp.bfloat16)
        return (
            jnp.einsum("kexb,kedb->exd", inner, right_sel, preferred_element_type=jnp.float32)
            * mask
        )

    start = psi_start[0] * mask
    start_sq = lax.psum(jnp.sum(start * start), "blk")
    vector = start / jnp.sqrt(start_sq)
    image = hamiltonian(vector)
    ritz_value = jnp.float32(0.0)
    for iteration in range(ITERS):
        rayleigh = lax.psum(jnp.sum(vector * image), "blk")
        resid = image - rayleigh * vector
        resid_sq = lax.psum(jnp.sum(resid * resid), "blk")
        coupling = jnp.sqrt(resid_sq + EPSILON)
        correction = resid / coupling
        corr_image = hamiltonian(correction)
        curvature = lax.psum(jnp.sum(correction * corr_image), "blk")
        ritz_value = 0.5 * (rayleigh + curvature) - jnp.sqrt(
            0.25 * (rayleigh - curvature) ** 2 + coupling * coupling
        )
        coef_old = curvature - ritz_value
        coef_new = -coupling
        length = jnp.sqrt(coef_old * coef_old + coef_new * coef_new)
        vector = (coef_old * vector + coef_new * correction) / length
        image = (coef_old * image + coef_new * corr_image) / length
    wave = (vector * (block_size * math.sqrt(entries * n_blocks))).astype(jnp.bfloat16)
    first = jnp.einsum("kexa,eab->kexb", left_sel, wave, preferred_element_type=jnp.float32).astype(
        jnp.bfloat16
    )
    left_term = (
        jnp.einsum("eax,keab->kexb", wave, first, preferred_element_type=jnp.float32) * inv_root
    ).astype(jnp.bfloat16)
    outgoing_terms = (
        jnp.zeros((channels, n_blocks * slot_count, block_size, block_size), jnp.bfloat16)
        .at[:, slot_mine]
        .set(left_term)
    )
    arrived = lax.all_to_all(outgoing_terms, "blk", split_axis=1, concat_axis=1, tiled=True)
    slot_hot = jnp.logical_and(
        slot_sector[:, None] == jnp.arange(sectors_dev)[None, :], slot_live[:, None]
    ).astype(jnp.bfloat16)
    left_sum = jnp.einsum("sj,ksxb->kjxb", slot_hot, arrived, preferred_element_type=jnp.float32)
    left_grown = jnp.einsum("kv,kjxb->vjxb", left_mix, left_sum, precision=hi).astype(jnp.bfloat16)
    second = jnp.einsum(
        "eab,kebd->kead", wave, right_sel, preferred_element_type=jnp.float32
    ).astype(jnp.bfloat16)
    right_term = (
        jnp.einsum("kead,ecd->keac", second, wave, preferred_element_type=jnp.float32) * inv_root
    )
    own_hot = (left_mine[:, None] == jnp.arange(sectors_dev)[None, :]).astype(jnp.float32)
    right_sum = jnp.einsum("ej,keac->kjac", own_hot, right_term, precision=hi)
    right_grown = jnp.einsum("kv,kjac->vjac", right_mix, right_sum, precision=hi).astype(
        jnp.bfloat16
    )
    return (wave[None], jnp.reshape(ritz_value, (1,)), left_grown[None], right_grown[None])


def solution(mesh):
    return jax.shard_map(
        body,
        mesh=mesh,
        in_specs=(
            P("sect", None, "blk", None, None),
            P("sect", None, "blk", None, None),
            P("sect", "blk", None, None),
            P("sect", None),
            P("sect", None, None),
            P("sect", None),
            P("sect", None),
            P("sect", None),
            P(),
            P(),
        ),
        out_specs=(
            P("sect", "blk", None, None),
            P("sect"),
            P("sect", None, "blk", None, None),
            P("sect", None, "blk", None, None),
        ),
        check_vma=False,
    )
```

profile of v0, /device:TPU:64, one launch (start us, length us, event | category | flops | bytes accessed | tf_op | source)
XLA Modules:
  0.0 1073.8 jit_solution(821274930283715342)
XLA Ops:
  5.9 21.9 %collective-permute-done.1 = bf16[1,17,4,128,128]{4,3,2,1,0:T(8,128)(2,1)S(1)} collective-permute-done((bf16[1,17,4,128,128]{4,3,2,1,0:T(8,128)(2,1)}, bf16[1,17,4,128,128]{4,3,2,1,0:T(8,128)(2,1)S(1)}, u32[]{:S(2)}, u32[]{:S(2)}) %collective-permute-start.1) | collective-permute-done | bytes 2228256 | tf_op jit(solution)/shard_map/ppermute | solution.py:17
  31.0 7.6 gather_fusion.1
  38.6 14.8 %select_bitcast_fusion = bf16[17,32,128,128]{3,2,0,1:T(8,128)(2,1)} fusion(bf16[32,17,128,128]{3,2,1,0:T(8,128)(2,1)} %gather_fusion.1, pred[32]{0:T(512)(128)(4,1)S(1)} %compare_and_fusion), kind=kLoop, calls=%fused_computation.10 | loop fusion | flops 8912896 | bytes 35651616 | tf_op jit(solution)/shard_map/jit(_take)/select_n | solution.py:89
  53.4 7.2 all-to-all-start
  60.7 3.3 collective-permute-start
  67.4 355.6 %psum.49 = f32[]{:T(128)} all-reduce(f32[]{:T(128)} %multiply_reduce_fusion.5), channel_id=1, replica_groups=mesh['sect'=8,'blk'=16] {'blk'}, use_global_device_ids=true, to_apply=%region_1.4 | all-reduce | flops 1 | bytes 8 | tf_op jit(solution)/shard_map/psum | solution.py:104
  425.7 6.4 gather_fusion
  432.1 12.5 %gather_fusion.2 = bf16[24,17,128,128]{3,2,1,0:T(8,128)(2,1)} fusion(bf16[17,32,128,128]{3,2,0,1:T(8,128)(2,1)} %all-to-all-done, s32[1024]{0:T(1024)S(1)} %pad_clamp_fusion), kind=kCustom, calls=%fused_computation.4 | custom fusion | bytes 26738784 | tf_op jit(solution)/shard_map/jit(_take)/gather | solution.py:91
  444.6 13.8 %multiply_reduce_fusion.4 = (f32[]{:T(128)}, f32[24,128,128]{2,1,0:T(8,128)S(1)}) fusion(f32[]{:T(128)S(6)} %sqrt.21, f32[1,24,128,128]{3,2,1,0:T(8,128)S(1)} %copy-done.4, pred[24,128]{1,0:T(8,128)(4,1)S(1)} %iota_compare_fusion.3, pred[24,128]{1,0:T(8,128)(4,1)S(1)} %iota_compare_fusion.4, bf16[24,17,128,128]{3,2,1,0:T(8,128)(2,1)} %gather_fusion.2, ...), kind=kOutput, calls=%fused_computation.67 | convolution fusion | flops 3446538240 | bytes 29890616 | tf_op jit(solution)/shard_map/kexb,kedb->exd/dot_general | solution.py:99
  458.4 36.1 %psum.50 = f32[]{:T(128)} all-reduce(f32[]{:T(128)} %get-tuple-element.46), channel_id=1, replica_groups=mesh['sect'=8,'blk'=16] {'blk'}, use_global_device_ids=true, to_apply=%region_5.8 | all-reduce | flops 1 | bytes 8 | tf_op jit(solution)/shard_map/psum | solution.py:109
  496.4 38.1 %psum.51 = f32[]{:T(128)} all-reduce(f32[]{:T(128)} %multiply_reduce_fusion.3), channel_id=1, replica_groups=mesh['sect'=8,'blk'=16] {'blk'}, use_global_device_ids=true, to_apply=%region_7.10 | all-reduce | flops 1 | bytes 8 | tf_op jit(solution)/shard_map/psum | solution.py:111
  535.1 15.9 %multiply_reduce_fusion.2 = (f32[]{:T(128)}, f32[24,128,128]{2,1,0:T(8,128)}) fusion(f32[]{:T(128)S(6)} %sqrt.22, f32[24,128,128]{2,1,0:T(8,128)S(1)} %get-tuple-element.47, f32[]{:T(128)} %psum.50, f32[]{:T(128)S(6)} %sqrt.21, f32[1,24,128,128]{3,2,1,0:T(8,128)S(1)} %copy-done.4, pred[24,128]{1,0:T(8,128)(4,1)S(1)} %iota_compare_fusion.3, ...), kind=kOutput, calls=%fused_computation.64 | convolution fusion | flops 3448897536 | bytes 31463488 | tf_op jit(solution)/shard_map/kexb,kedb->exd/dot_general | solution.py:99
  551.0 36.1 %psum.52 = f32[]{:T(128)} all-reduce(f32[]{:T(128)} %get-tuple-element.48), channel_id=1, replica_groups=mesh['sect'=8,'blk'=16] {'blk'}, use_global_device_ids=true, to_apply=%region_9.12 | all-reduce | flops 1 | bytes 8 | tf_op jit(solution)/shard_map/psum | solution.py:115
  590.4 5.5 multiply_reduce_fusion.1
  595.9 38.6 %psum.53 = f32[]{:T(128)} all-reduce(f32[]{:T(128)} %get-tuple-element.37), channel_id=1, replica_groups=mesh['sect'=8,'blk'=16] {'blk'}, use_global_device_ids=true, to_apply=%region_11.14 | all-reduce | flops 1 | bytes 8 | tf_op jit(solution)/shard_map/psum | solution.py:109
  634.5 3.1 multiply_reduce_fusion
  637.6 36.1 %psum.54 = f32[]{:T(128)} all-reduce(f32[]{:T(128)} %multiply_reduce_fusion), channel_id=1, replica_groups=mesh['sect'=8,'blk'=16] {'blk'}, use_global_device_ids=true, to_apply=%region_13.16 | all-reduce | flops 1 | bytes 8 | tf_op jit(solution)/shard_map/psum | solution.py:111
  674.4 14.6 %fusion.71 = f32[]{:T(128)} fusion(pred[24,128]{1,0:T(8,128)(4,1)S(1)} %iota_compare_fusion.3, pred[24,128]{1,0:T(8,128)(4,1)S(1)} %iota_compare_fusion.4, f32[]{:T(128)S(6)} %sqrt.25, f32[24,128,128]{2,1,0:T(8,128)S(1)} %get-tuple-element.38, f32[24,128,128]{2,1,0:T(8,128)S(1)} %copy-done.5, f32[]{:T(128)} %psum.53, ...), kind=kOutput, calls=%fused_computation.57 | convolution fusion | flops 3446931456 | bytes 29890620 | tf_op jit(solution)/shard_map/kexb,kedb->exd/dot_general | solution.py:99
  689.0 38.1 %psum.55 = f32[]{:T(128)} all-reduce(f32[]{:T(128)} %fusion.71), channel_id=1, replica_groups=mesh['sect'=8,'blk'=16] {'blk'}, use_global_device_ids=true, to_apply=%region_15.18 | all-reduce | flops 1 | bytes 8 | tf_op jit(solution)/shard_map/psum | solution.py:115
  732.4 15.4 %fusion.2 = bf16[24,17,128,128]{2,3,1,0:T(8,128)(2,1)} fusion(bf16[24,128,128]{2,1,0:T(8,128)(2,1)} %multiply_convert_fusion.1, bf16[24,17,128,128]{3,2,1,0:T(8,128)(2,1)} %gather_fusion, pred[24]{0:T(512)(128)(4,1)S(1)} %get-tuple-element.42), kind=kOutput, calls=%fused_computation.11 | convolution fusion | flops 3449290752 | bytes 27525144 | tf_op jit(solution)/shard_map/eax,keab->kexb/dot_general | solution.py:129
  747.8 18.3 %copy.67 = bf16[24,17,128,128]{3,2,1,0:T(8,128)(2,1)} copy(bf16[24,17,128,128]{2,3,1,0:T(8,128)(2,1)} %fusion.2) | data formatting | bytes 26738688 | tf_op jit(solution)/shard_map/convert_element_type | solution.py:130
  766.1 6.6 broadcast_in_dim.108
  772.7 32.0 %scatter_fusion = bf16[17,32,128,128]{3,2,1,0:T(8,128)(2,1)} fusion(bf16[17,32,128,128]{3,2,1,0:T(8,128)(2,1)} %broadcast_in_dim.108, s32[24]{0:T(128)S(1)} %get-tuple-element.41, bf16[24,17,128,128]{3,2,1,0:T(8,128)(2,1)} %copy.67), kind=kCustom, calls=%fused_computation.5 | custom fusion | bytes 40108128 | tf_op jit(solution)/shard_map/scatter | solution.py:134
  804.7 14.8 %copy.68 = bf16[17,32,128,128]{3,2,0,1:T(8,128)(2,1)} copy(bf16[17,32,128,128]{3,2,1,0:T(8,128)(2,1)} %scatter_fusion) | data formatting | bytes 35651584 | tf_op jit(solution)/shard_map/scatter | solution.py:134
  819.5 5.5 all-to-all-start.1
  825.3 16.8 %multiply_bitcast_fusion = f32[17,24,128,128]{2,3,0,1:T(8,128)} fusion(bf16[24,128,128]{2,1,0:T(8,128)(2,1)S(1)} %copy-done.6, bf16[24,17,128,128]{3,2,1,0:T(8,128)(2,1)} %gather_fusion.2, pred[24]{0:T(512)(128)(4,1)S(1)} %get-tuple-element.40), kind=kOutput, calls=%fused_computation.6 | convolution fusion | flops 3442606080 | bytes 40894488 | tf_op jit(solution)/shard_map/kead,ecd->keac/dot_general | solution.py:146
  842.1 27.2 %copy.75 = f32[17,24,128,128]{3,1,2,0:T(8,128)} copy(f32[17,24,128,128]{2,3,0,1:T(8,128)} %multiply_bitcast_fusion) | data formatting | bytes 53477376 | tf_op jit(solution)/shard_map/mul | solution.py:146
  869.4 14.7 %convolution_bitcast_fusion = f32[17,4,128,128]{3,1,2,0:T(4,128)S(1)} fusion(f32[17,24,128,128]{3,1,2,0:T(8,128)} %copy.75, s32[24]{0:T(128)S(1)} %copy-done.13), kind=kOutput, calls=%fused_computation.55 | convolution fusion | flops 320864352 | bytes 31195232 | tf_op jit(solution)/shard_map/ej,keac->kjac/dot_general | solution.py:149
  884.1 8.9 convert_bitcast_fusion
  894.9 150.4 %all-to-all-done.1 = bf16[17,32,128,128]{3,2,0,1:T(8,128)(2,1)} async-done(((bf16[17,32,128,128]{3,2,0,1:T(8,128)(2,1)}), bf16[17,32,128,128]{3,2,0,1:T(8,128)(2,1)}, u32[]{:S(2)}, u32[]{:S(2)}) %all-to-all-start.1) | async-done | bytes 17825824 | tf_op jit(solution)/shard_map/all_to_all | solution.py:136
  1045.3 16.0 %fusion.67 = f32[17,4,128,128]{3,1,2,0:T(4,128)S(1)} fusion(bf16[17,32,128,128]{3,2,0,1:T(8,128)(2,1)} %all-to-all-done.1, s32[32]{0:T(128)S(1)} %copy-done.15, pred[32]{0:T(512)(128)(4,1)S(1)} %and.77), kind=kOutput, calls=%fused_computation.54 | convolution fusion | flops 71303424 | bytes 22282400 | tf_op jit(solution)/shard_map/sj,ksxb->kjxb/dot_general | solution.py:140
  1061.3 8.9 convert_bitcast_fusion.1
  (78 shorter events, 21.9 us)
Async XLA Ops:
  0.6 883.4 %copy-start = (f32[17,17]{1,0:T(8,128)S(1)}, f32[17,17]{1,0:T(8,128)}, u32[]{:S(2)}) copy-start(f32[17,17]{1,0:T(8,128)} %param.23) | copy-start | bytes 3472
  0.6 27.2 %collective-permute-start.1 = (bf16[1,17,4,128,128]{4,3,2,1,0:T(8,128)(2,1)}, bf16[1,17,4,128,128]{4,3,2,1,0:T(8,128)(2,1)S(1)}, u32[]{:S(2)}, u32[]{:S(2)}) collective-permute-start(bf16[1,17,4,128,128]{4,3,2,1,0:T(8,128)(2,1)} %param.15), channel_id=1, source_target_pairs={{16,0},{32,16},{48,32},{64,48},{80,64},{96,80},{112,96},{17,1},{33... | collective-permute-start | bytes 6684680 | tf_op jit(solution)/shard_map/ppermute | solution.py:17
  4.6 0.6 copy-start.9
  5.6 25.4 %copy-start.14 = (s32[32]{0:T(128)}, s32[32]{0:T(128)S(1)}, u32[]{:S(2)}) copy-start(s32[32]{0:T(128)S(1)} %reshape.192) | copy-start | bytes 388
  27.8 1.4 copy-start.8
  53.4 10.5 copy-start.16
  53.4 11.2 %copy-start.1 = (s32[1,64]{1,0:T(1,128)S(1)}, s32[1,64]{1,0:T(1,128)}, u32[]{:S(2)}) copy-start(s32[1,64]{1,0:T(1,128)} %param.21) | copy-start | bytes 772
  53.4 11.9 %copy-start.2 = (s32[1,64]{1,0:T(1,128)S(1)}, s32[1,64]{1,0:T(1,128)}, u32[]{:S(2)}) copy-start(s32[1,64]{1,0:T(1,128)} %param.20) | copy-start | bytes 772
  53.4 12.8 %copy-start.3 = (f32[1,24,128,128]{3,2,1,0:T(8,128)S(1)}, f32[1,24,128,128]{3,2,1,0:T(8,128)}, u32[]{:S(2)}) copy-start(f32[1,24,128,128]{3,2,1,0:T(8,128)} %param.16) | copy-start | bytes 4718596
  53.4 378.6 %all-to-all-start = ((bf16[17,32,128,128]{3,2,0,1:T(8,128)(2,1)}), bf16[17,32,128,128]{3,2,0,1:T(8,128)(2,1)}, u32[]{:S(2)}, u32[]{:S(2)}) async-start(bf16[17,32,128,128]{3,2,0,1:T(8,128)(2,1)} %select_bitcast_fusion), calls=%async_computation | async-start | bytes 35651584 | tf_op jit(solution)/shard_map/all_to_all | solution.py:90
  60.7 363.2 %collective-permute-start = (bf16[1,17,4,128,128]{4,3,2,1,0:T(8,128)(2,1)}, bf16[1,17,4,128,128]{4,3,2,1,0:T(8,128)(2,1)}, u32[]{:S(2)}, u32[]{:S(2)}) collective-permute-start(bf16[1,17,4,128,128]{4,3,2,1,0:T(8,128)(2,1)} %param.14), channel_id=1, source_target_pairs={{0,16},{16,32},{32,48},{48,64},{64,80},{80,96},{96,112},{1,17},{17... | collective-permute-start | bytes 6684680 | tf_op jit(solution)/shard_map/ppermute | solution.py:17
  64.0 0.6 copy-start.12
  432.1 12.5 %copy-start.4 = (f32[1,24,128,128]{3,2,1,0:T(8,128)S(1)}, f32[1,24,128,128]{3,2,1,0:T(8,128)}, u32[]{:S(2)}) copy-start(f32[1,24,128,128]{3,2,1,0:T(8,128)} %param.16) | copy-start | bytes 4718596
  458.4 92.6 %copy-start.7 = (f32[24,128,128]{2,1,0:T(8,128)}, f32[24,128,128]{2,1,0:T(8,128)S(1)}, u32[]{:S(2)}) copy-start(f32[24,128,128]{2,1,0:T(8,128)S(1)} %get-tuple-element.47) | copy-start | bytes 4718596
  595.9 78.4 %copy-start.5 = (f32[24,128,128]{2,1,0:T(8,128)S(1)}, f32[24,128,128]{2,1,0:T(8,128)}, u32[]{:S(2)}) copy-start(f32[24,128,128]{2,1,0:T(8,128)} %get-tuple-element.39) | copy-start | bytes 4718596
  819.5 5.5 copy-start.10
  819.5 5.9 copy-start.6
  819.5 225.8 %all-to-all-start.1 = ((bf16[17,32,128,128]{3,2,0,1:T(8,128)(2,1)}), bf16[17,32,128,128]{3,2,0,1:T(8,128)(2,1)}, u32[]{:S(2)}, u32[]{:S(2)}) async-start(bf16[17,32,128,128]{3,2,0,1:T(8,128)(2,1)} %copy.68), calls=%async_computation.1 | async-start | bytes 35651584 | tf_op jit(solution)/shard_map/all_to_all | solution.py:136
  842.1 27.2 %copy-start.13 = (s32[24]{0:T(128)S(1)}, s32[24]{0:T(128)}, u32[]{:S(2)}) copy-start(s32[24]{0:T(128)} %copy-done.12) | copy-start | bytes 292
  893.0 152.3 %copy-start.15 = (s32[32]{0:T(128)S(1)}, s32[32]{0:T(128)}, u32[]{:S(2)}) copy-start(s32[32]{0:T(128)} %copy-done.14) | copy-start | bytes 388
  894.9 166.4 %copy-start.11 = (f32[17,17]{1,0:T(8,128)S(1)}, f32[17,17]{1,0:T(8,128)}, u32[]{:S(2)}) copy-start(f32[17,17]{1,0:T(8,128)} %param.22) | copy-start | bytes 3472
where the time goes:
time: 1090 us; the launch traced here: 1070 us
  blocking collectives  579 us (53%)
  waiting for transfers between devices  172 us (16%)
  local copies, waits for them, and re-layouts  134 us (12%)
  matrix products  125 us (11%)
  other arithmetic  34.8 us (3%)
  starting transfers between devices  17.9 us (2%)
  between operations  11.3 us (1%)
    psum x1, blocking collectives, body(): start_sq = lax.psum(jnp.sum(start * start), 'blk')  356 us
    all_to_all x1, waiting for transfers between devices, body(): lax.all_to_all(outgoing_terms, 'blk', split_axis=1, concat_axis=1, tiled=...  150 us
    psum x2, blocking collectives, body(): rayleigh = lax.psum(jnp.sum(vector * image), 'blk')  74.7 us
    psum x2, blocking collectives, body(): curvature = lax.psum(jnp.sum(correction * corr_image), 'blk')  74.1 us
    psum x2, blocking collectives, body(): resid_sq = lax.psum(jnp.sum(resid * resid), 'blk')  74.1 us
    scatter x2, local copies, waits for them, and re-layouts, body(): outgoing_terms = jnp.zeros((channels, n_blocks * slot_count, block_size,...  46.8 us
    dot_general x3, matrix products, hamiltonian(): jnp.einsum('kexb,kedb->exd', inner, right_sel, preferred_element_type=jnp...  44.2 us
    mul x1, local copies, waits for them, and re-layouts, body(): jnp.einsum('kead,ecd->keac', second, wave, preferred_element_type=jnp.flo...  27.2 us
  transfers between devices with their start and end apart: 4, of which 2 were waited for; matrix products, arithmetic and copies ran while one was open for 8% of the time, Pallas kernels for 0%

commit v1 on v0

v1 whole, which is shorter than its diff:
```python
import math

import jax
import jax.numpy as jnp
from jax import lax
from jax.experimental import pallas as pl
from jax.experimental.pallas import tpu as pltpu
from jax.sharding import PartitionSpec as P

MESH = pl.DeviceIdType.MESH
F32 = jnp.float32
BF16 = jnp.bfloat16
EPSILON = 1e-06

N = 128
HALF = 64
SIDE = 4
SEC = 4
RANKS = 2
SLOTS = SIDE * SIDE * RANKS
RUN = 24
PACK = SEC * HALF + 16
UNROLL = 4
LAG = 2

SEND, SLOT_OF, LSEC, RSEC, LDIM, RDIM = 0, 32, 64, 96, 128, 160
ORD_R, KEEP_R, LAST_R, LIVE_R = 192, 224, 256, 272
ORD_L, KEEP_L, LAST_L, LIVE_L = 288, 320, 352, 368
TABLE = 384


def router(left_local, right_group, right_local, left_dims, right_dims, table, count):
    me = lax.axis_index("blk")
    my_x, my_y = me >> 2, me & 3

    def clear(i, _):
        table[SEND + i] = 0
        table[SLOT_OF + i] = 0
        table[LSEC + i] = (i >> 3) * SEC
        table[RSEC + i] = ((i & 7) >> 1) * SEC
        table[LDIM + i] = 0
        table[RDIM + i] = 0
        return 0

    lax.fori_loop(0, SLOTS, clear, 0)

    def zero_counts():
        for i in range(SIDE * SIDE):
            count[i] = 0

    zero_counts()

    def own(e, _):
        group = right_group[me * RUN + e]
        rank = jnp.minimum(count[group], RANKS - 1)
        count[group] = rank + 1
        slot = (group & 3) * 8 + (group >> 2) * 2 + rank
        table[SLOT_OF + e] = slot
        table[SEND + slot] = e
        return 0

    lax.fori_loop(0, RUN, own, 0)
    for source in range(SIDE):
        run = my_x * SIDE + source
        zero_counts()

        def other(e, _):
            at = run * RUN + e
            group = right_group[at]
            rank = jnp.minimum(count[group], RANKS - 1)
            count[group] = rank + 1

            @pl.when((group & 3) == my_y)
            def _():
                slot = source * 8 + (group >> 2) * 2 + rank
                left, right = left_local[at], right_local[at]
                table[LSEC + slot] = source * SEC + left
                table[RSEC + slot] = (group >> 2) * SEC + right
                table[LDIM + slot] = left_dims[run * SEC + left]
                table[RDIM + slot] = right_dims[group * SEC + right]

            return 0

        lax.fori_loop(0, RUN, other, 0)
    for key, order, keep, last, live in (
        (LSEC, ORD_R, KEEP_R, LAST_R, LIVE_R),
        (RSEC, ORD_L, KEEP_L, LAST_L, LIVE_L),
    ):
        zero_counts()

        def tally(s, _):
            sector = table[key + s]
            count[sector] = count[sector] + 1
            return 0

        lax.fori_loop(0, SLOTS, tally, 0)
        for g in range(SIDE):
            begin = jnp.int32(0)
            for j in range(SEC):
                sector = g * SEC + j
                amount = count[sector]
                count[sector] = g * 8 + begin
                table[live + sector] = jnp.minimum(amount, 1)
                begin = begin + amount
                table[last + sector] = jnp.maximum(begin - 1, 0)

        def place(s, _):
            sector = table[key + s]
            at = count[sector]
            count[sector] = at + 1
            table[order + at] = s
            return 0

        lax.fori_loop(0, SLOTS, place, 0)

        def compare(p, _):
            before = table[order + jnp.maximum(p - 1, 0)]
            same = table[key + table[order + p]] == table[key + before]
            table[keep + p] = jnp.where(jnp.logical_and((p & 7) != 0, same), 1, 0)
            return 0

        lax.fori_loop(0, SLOTS, compare, 0)


def dot(a, b):
    return jnp.dot(a, b, preferred_element_type=F32)


def triangle_masks():
    row = lax.broadcasted_iota(jnp.int32, (HALF, N), 0)
    col = lax.broadcasted_iota(jnp.int32, (HALF, N), 1)
    left = col < HALF
    below = jnp.logical_and(left, row > col)
    low = jnp.logical_and(col >= HALF, row > col - HALF)
    high = jnp.logical_and(col >= HALF, row < col - HALF)
    diag = row == col - HALF
    return below, left, low, high, diag


def pack(block, masks):
    below, _, _, _, diag = masks
    corner = block[HALF:]
    upper = jnp.where(below, pltpu.roll(corner, HALF, 1), block[:HALF])
    row = jnp.sum(jnp.where(diag, corner, 0.0), axis=0, keepdims=True)
    return upper, row


def unpack(packed, row, masks):
    below, above, left, low, high, diag = masks
    turned = jnp.concatenate([packed, packed], axis=0).T
    rolled = pltpu.roll(packed.astype(F32), HALF, 1).astype(BF16)
    top = packed * above + turned[:HALF] * below
    bottom = (
        turned[HALF:] * left
        + rolled * low
        + turned[:HALF] * high
        + jnp.broadcast_to(row, (HALF, N)).astype(BF16) * diag
    )
    return jnp.concatenate([top, bottom], axis=0)


def kernel(
    channels,
    table,
    left_mix,
    right_mix,
    left_hbm,
    right_hbm,
    psi,
    wave,
    energy,
    left_out,
    right_out,
    bound,
    cat,
    gath,
    outb,
    work,
    vec,
    vect,
    ret,
    stack,
    red,
    mine,
    local_sem,
    psi_send,
    psi_recv,
    z_send,
    z_recv,
    ring_send,
    ring_recv,
    red_send,
    red_recv,
    grow_send,
    grow_recv,
):
    n_sect = lax.axis_size("sect")
    sect = lax.axis_index("sect")
    me = lax.axis_index("blk")
    my_x, my_y = me // SIDE, me % SIDE
    up, down = (sect + 1) % n_sect, (sect + n_sect - 1) % n_sect
    half = channels // 2

    def along_y(step):
        return my_x * SIDE + (my_y + step) % SIDE

    def along_x(step):
        return ((my_x + step) % SIDE) * SIDE + my_y

    barrier = pltpu.get_barrier_semaphore()

    def greet(d, _):
        pl.semaphore_signal(
            barrier, inc=1, device_id={"blk": (me + d) % (SIDE * SIDE)}, device_id_type=MESH
        )
        return 0

    lax.fori_loop(1, SIDE * SIDE, greet, 0)
    pl.semaphore_signal(barrier, inc=1, device_id={"sect": up}, device_id_type=MESH)
    pl.semaphore_signal(barrier, inc=1, device_id={"sect": down}, device_id_type=MESH)

    loads = [
        pltpu.make_async_copy(left_hbm, bound.at[0], local_sem.at[0]),
        pltpu.make_async_copy(right_hbm, bound.at[1], local_sem.at[1]),
    ]
    for load in loads:
        load.start()

    def fill(i, _):
        ret[i] = psi[table[SEND + i]].astype(BF16)
        return 0

    lax.fori_loop(0, SLOTS, fill, 0)
    pl.semaphore_wait(barrier, SIDE * SIDE + 1)

    def psi_copy(step):
        to_y = (my_y + step) % SIDE
        return pltpu.make_async_remote_copy(
            src_ref=ret.at[pl.ds(to_y * 8, 8)],
            dst_ref=vec.at[pl.ds(my_y * 8, 8)],
            send_sem=psi_send.at[step - 1],
            recv_sem=psi_recv.at[step - 1],
            device_id={"blk": along_y(step)},
            device_id_type=MESH,
        )

    for step in (1, 3, 2):
        psi_copy(step).start()

    masks = triangle_masks()
    below, left, low, high, diag = masks
    ones = [jnp.where(m, 1.0, 0.0).astype(BF16) for m in (below, left, low, high, diag)]
    bits = (ones[0], jnp.where(below, 0.0, 1.0).astype(BF16), ones[1], ones[2], ones[3], ones[4])
    row16 = lax.broadcasted_iota(jnp.int32, (16, N), 0)
    eye_packed = jnp.where(
        lax.broadcasted_iota(jnp.int32, (HALF, N), 0) == lax.broadcasted_iota(jnp.int32, (HALF, N), 1),
        1.0,
        0.0,
    )
    eye_row = jnp.where(lax.broadcasted_iota(jnp.int32, (1, N), 1) >= HALF, 1.0, 0.0)

    def place(side):
        return my_y if side == 0 else my_x

    def z_copy(side, k):
        return pltpu.make_async_remote_copy(
            src_ref=outb.at[side, 3, k],
            dst_ref=gath.at[side, place(side), k],
            send_sem=z_send.at[side, k],
            recv_sem=z_recv.at[side, k],
            device_id={"sect": up if side == 0 else down},
            device_id_type=MESH,
        )

    for load in loads:
        load.wait()

    def pack_bound(k, _):
        for side in range(2):
            edge = sect == (n_sect - 1 if side == 0 else 0)
            here = k == (0 if side == 0 else channels - 1)
            rows = jnp.zeros((16, N), F32)
            for j in range(SEC):
                upper, row = pack(bound[side, k, j].astype(F32), masks)
                one = jnp.where(here, 1.0, 0.0)
                upper = jnp.where(edge, eye_packed * one, upper)
                row = jnp.where(edge, eye_row * one, row)
                outb[side, 3, k, pl.ds(j * HALF, HALF)] = upper.astype(BF16)
                rows = jnp.where(row16 == j, jnp.broadcast_to(row, (16, N)), rows)
            outb[side, 3, k, pl.ds(SEC * HALF, 16)] = rows.astype(BF16)
            z_copy(side, k).start()
        return 0

    lax.fori_loop(0, channels, pack_bound, 0)

    def ring_copy(side, which, k, back):
        at = place(side)
        if which == 2:
            at = (at + (1 if back else SIDE - 1)) % SIDE
        step = SIDE - 1 if back else 1
        return pltpu.make_async_remote_copy(
            src_ref=gath.at[side, at, k],
            dst_ref=gath.at[side, at, k],
            send_sem=ring_send.at[side, which, k],
            recv_sem=ring_recv.at[side, which, k],
            device_id={"blk": along_y(step) if side == 0 else along_x(step)},
            device_id_type=MESH,
        )

    def dims_mask(slot):
        rows = lax.broadcasted_iota(jnp.int32, (N, N), 0) < table[LDIM + slot]
        cols = lax.broadcasted_iota(jnp.int32, (N, N), 1) < table[RDIM + slot]
        return jnp.logical_and(rows, cols)

    X, HX, T, HT = 0, SLOTS, 2 * SLOTS, 3 * SLOTS

    def gather_step(t, _):
        @pl.when(t < channels)
        def _():
            for side in range(2):
                z_copy(side, t).wait_recv()
                ring_copy(side, 0, t, False).start()
                ring_copy(side, 1, t, True).start()

        @pl.when(jnp.logical_and(t >= 1, t < channels + 1))
        def _():
            k = t - 1
            for side in range(2):
                ring_copy(side, 0, k, False).wait_recv()
                ring_copy(side, 1, k, True).wait_recv()

            @pl.when(k % 2 == 0)
            def _():
                for side in range(2):
                    ring_copy(side, 2, k, False).start()

            @pl.when(k % 2 == 1)
            def _():
                for side in range(2):
                    ring_copy(side, 2, k, True).start()

        @pl.when(t == LAG)
        def _():
            for step in (1, 3, 2):
                psi_copy(step).wait_recv()
            for i in range(8):
                vec[my_y * 8 + i] = ret[my_y * 8 + i]

            def start(i, _):
                vec[i] = jnp.where(dims_mask(i), vec[i].astype(F32), 0.0).astype(BF16)
                work[HX + i] = jnp.zeros((N, N), F32)
                return 0

            lax.fori_loop(0, SLOTS, start, 0)

        @pl.when(t >= LAG)
        def _():
            k = t - LAG
            for side in range(2):
                ring_copy(side, 2, k, False).wait_recv()

            def open_group(g, _):
                for side in range(2):
                    rows = gath[side, g, k, pl.ds(SEC * HALF, 16)].astype(F32)
                    for j in range(SEC):
                        row = jnp.sum(jnp.where(row16 == j, rows, 0.0), axis=0, keepdims=True)
                        packed = gath[side, g, k, pl.ds(j * HALF, HALF)]
                        cat[side, g * SEC + j, k] = unpack(packed, row, bits)
                return 0

            lax.fori_loop(0, SIDE, open_group, 0)

            def apply(i, _):
                slots = [i * UNROLL + u for u in range(UNROLL)]
                inner = [dot(vec[s], cat[1, table[RSEC + s], k]).astype(BF16) for s in slots]
                for s, z in zip(slots, inner):
                    work[HX + s] += dot(cat[0, table[LSEC + s], k], z)
                return 0

            lax.fori_loop(0, SLOTS // UNROLL, apply, 0)

        return 0

    lax.fori_loop(0, channels + LAG, gather_step, 0)

    for step in (1, 3, 2):
        psi_copy(step).wait_send()

    def settle(k, _):
        for side in range(2):
            z_copy(side, k).wait_send()
            for which in range(3):
                ring_copy(side, which, k, False).wait_send()
        return 0

    lax.fori_loop(0, channels, settle, 0)

    def fold(block):
        return jnp.sum(block.reshape(N // 8, 8, N), axis=0)

    def exchange(number, parts):
        rows = [jnp.sum(p, axis=0, keepdims=True) for p in parts]
        rows += [jnp.zeros((1, N), F32)] * (8 - len(rows))
        mine[number] = jnp.concatenate(rows, axis=0)

        def copy(d):
            return pltpu.make_async_remote_copy(
                src_ref=mine.at[number],
                dst_ref=red.at[number, me],
                send_sem=red_send.at[number, d],
                recv_sem=red_recv.at[number, d],
                device_id={"blk": (me + d) % (SIDE * SIDE)},
                device_id_type=MESH,
            )

        def begin(d, _):
            copy(d).start()
            return 0

        lax.fori_loop(1, SIDE * SIDE, begin, 0)
        red[number, me] = mine[number]

        def end(d, _):
            copy(d).wait()
            return 0

        lax.fori_loop(1, SIDE * SIDE, end, 0)
        total = jnp.sum(red[number], axis=0)
        total = jnp.broadcast_to(jnp.sum(total, axis=1, keepdims=True), (8, N))
        return [total[i : i + 1] for i in range(len(parts))]

    zero8 = jnp.zeros((8, N), F32)

    def first_sums(s, sums):
        ss, sh, hh = sums
        start = vec[s].astype(F32)
        image = jnp.where(dims_mask(s), work[HX + s], 0.0)
        work[HX + s] = image
        return ss + fold(start * start), sh + fold(start * image), hh + fold(image * image)

    ss, sh, hh = exchange(0, lax.fori_loop(0, SLOTS, first_sums, (zero8,) * 3))
    norm = jnp.sqrt(ss)
    xx = ss / (norm * norm)
    a = sh / (norm * norm)
    hxhx = hh / (norm * norm)
    b = jnp.sqrt(jnp.maximum(hxhx - 2.0 * a * a + a * a * xx, 0.0) + EPSILON)

    def first_residual(s, _):
        x = vec[s].astype(F32) / norm
        hx = work[HX + s] / norm
        t = (hx - a * x) / b
        work[X + s] = x
        work[HX + s] = hx
        work[T + s] = t
        vec[s] = t.astype(BF16)
        return 0

    lax.fori_loop(0, SLOTS, first_residual, 0)

    def beside(side, sector):
        return jnp.concatenate([cat[side, sector, k] for k in range(channels)], axis=1)

    def hamiltonian(i, _):
        slots = [i * UNROLL + u for u in range(UNROLL)]
        inner = []
        for s in slots:
            z = dot(vec[s], beside(1, table[RSEC + s])).astype(BF16)
            inner.append(jnp.concatenate([z[:, k * N : (k + 1) * N] for k in range(channels)], axis=0))
        for s, z in zip(slots, inner):
            work[HT + s] = jnp.where(dims_mask(s), dot(beside(0, table[LSEC + s]), z), 0.0)
        return 0

    lax.fori_loop(0, SLOTS // UNROLL, hamiltonian, 0)

    def second_sums(s, sums):
        x, hx, t, ht = work[X + s], work[HX + s], work[T + s], work[HT + s]
        terms = (x * t, t * t, x * ht, t * hx, t * ht, hx * ht, ht * ht)
        return tuple(old + fold(term) for old, term in zip(sums, terms))

    xt, tt, xht, thx, c, hxht, htht = exchange(
        1, lax.fori_loop(0, SLOTS, second_sums, (zero8,) * 7)
    )

    def ritz(a, b, c):
        value = 0.5 * (a + c) - jnp.sqrt(0.25 * (a - c) * (a - c) + b * b)
        old, new = c - value, -b
        length = jnp.sqrt(old * old + new * new)
        return value, old / length, new / length

    _, p, q = ritz(a, b, c)
    a2 = p * p * a + p * q * (xht + thx) + q * q * c
    xx2 = p * p * xx + 2.0 * p * q * xt + q * q * tt
    hxhx2 = p * p * hxhx + 2.0 * p * q * hxht + q * q * htht
    b2 = jnp.sqrt(jnp.maximum(hxhx2 - 2.0 * a2 * a2 + a2 * a2 * xx2, 0.0) + EPSILON)

    def second_residual(s, _):
        x = p * work[X + s] + q * work[T + s]
        hx = p * work[HX + s] + q * work[HT + s]
        t = (hx - a2 * x) / b2
        work[X + s] = x
        work[T + s] = t
        vec[s] = t.astype(BF16)
        return 0

    lax.fori_loop(0, SLOTS, second_residual, 0)
    lax.fori_loop(0, SLOTS // UNROLL, hamiltonian, 0)

    def third_sums(s, total):
        return total + fold(work[T + s] * work[HT + s])

    (c2,) = exchange(2, [lax.fori_loop(0, SLOTS, third_sums, zero8)])
    value, p2, q2 = ritz(a2, b2, c2)
    energy[...] = jnp.broadcast_to(value, (8, N))
    scale = N * math.sqrt(RUN * SIDE * SIDE)

    def final_vector(s, _):
        w = ((p2 * work[X + s] + q2 * work[T + s]) * scale).astype(BF16)
        vec[s] = w
        vect[s] = w.T
        return 0

    lax.fori_loop(0, SLOTS, final_vector, 0)

    def wave_copy(step):
        to_y = (my_y + step) % SIDE
        return pltpu.make_async_remote_copy(
            src_ref=vec.at[pl.ds(to_y * 8, 8)],
            dst_ref=ret.at[pl.ds(my_y * 8, 8)],
            send_sem=psi_send.at[step + 2],
            recv_sem=psi_recv.at[step + 2],
            device_id={"blk": along_y(step)},
            device_id_type=MESH,
        )

    def grow(kind, group, to):
        order, keep, last, live = (
            (ORD_L, KEEP_L, LAST_L, LIVE_L) if kind == 0 else (ORD_R, KEEP_R, LAST_R, LIVE_R)
        )
        outer, sector_at = (vect, LSEC) if kind == 0 else (vec, RSEC)
        closing = vec if kind == 0 else vect

        def term(i, _):
            spots = [i * 2 + u for u in range(2)]
            for u, spot in enumerate(spots):
                slot = table[order + group * 8 + spot]
                z = dot(outer[slot], beside(kind, table[sector_at + slot])).astype(BF16)
                for k in range(channels):
                    stack[u, k] = z[:, k * N : (k + 1) * N]
            for u, spot in enumerate(spots):
                slot = table[order + group * 8 + spot]
                stay = table[keep + group * 8 + spot] > 0
                right = closing[slot]
                for k in range(channels):
                    before = work[jnp.maximum(spot - 1, 0) * channels + k]
                    work[spot * channels + k] = dot(stack[u, k], right) + jnp.where(stay, before, 0.0)
            return 0

        lax.fori_loop(0, 4, term, 0)

        def close(k, _):
            rows = jnp.zeros((16, N), F32)
            for j in range(SEC):
                spot = table[last + group * SEC + j]
                has = table[live + group * SEC + j] > 0
                upper, row = pack(work[spot * channels + k], masks)
                outb[kind, to, k, pl.ds(j * HALF, HALF)] = jnp.where(has, upper, 0.0).astype(BF16)
                row = jnp.where(has, row, 0.0)
                rows = jnp.where(row16 == j, jnp.broadcast_to(row, (16, N)), rows)
            outb[kind, to, k, pl.ds(SEC * HALF, 16)] = rows.astype(BF16)
            return 0

        lax.fori_loop(0, channels, close, 0)

    first, second = pl.ds(0, half), pl.ds(half, channels - half)

    def grow_copy(kind, number):
        source, target, part, back = (
            (0, 0, first, False),
            (0, 0, second, True),
            (1, 1, second, False),
            (1, 1, first, False),
            (2, 2, first, True),
            (2, 2, second, True),
        )[number]
        step = SIDE - 1 if back else 1
        return pltpu.make_async_remote_copy(
            src_ref=outb.at[kind, source, part],
            dst_ref=gath.at[kind, target, part],
            send_sem=grow_send.at[kind, number],
            recv_sem=grow_recv.at[kind, number],
            device_id={"blk": along_x(step) if kind == 0 else along_y(step)},
            device_id_type=MESH,
        )

    def my_group(kind, step):
        return ((my_x if kind == 0 else my_y) + step) % SIDE

    for kind in range(2):
        grow(kind, my_group(kind, 2), 0)
        grow_copy(kind, 0).start()
        grow_copy(kind, 1).start()
    for kind in range(2):
        grow(kind, my_group(kind, 1), 1)
        grow_copy(kind, 2).start()
    for step in (1, 3, 2):
        wave_copy(step).start()
    for kind in range(2):
        grow(kind, my_group(kind, SIDE - 1), 2)
        grow_copy(kind, 4).start()
    for kind in range(2):
        grow_copy(kind, 0).wait_recv()

        def add_first(k, _):
            outb[kind, 1, k] = (outb[kind, 1, k].astype(F32) + gath[kind, 0, k].astype(F32)).astype(BF16)
            return 0

        lax.fori_loop(0, half, add_first, 0)
        grow_copy(kind, 3).start()
        grow_copy(kind, 1).wait_recv()

        def add_second(k, _):
            outb[kind, 2, k] = (outb[kind, 2, k].astype(F32) + gath[kind, 0, k].astype(F32)).astype(BF16)
            return 0

        lax.fori_loop(half, channels, add_second, 0)
        grow_copy(kind, 5).start()
    for kind in range(2):
        grow(kind, my_group(kind, 0), 3)

    for step in (1, 3, 2):
        wave_copy(step).wait_recv()
    for i in range(8):
        ret[my_y * 8 + i] = vec[my_y * 8 + i]

    def take(e, _):
        wave[e] = ret[table[SLOT_OF + e]]
        return 0

    lax.fori_loop(0, RUN, take, 0)

    shrink = 1.0 / math.sqrt(N)
    stores = []
    for kind in range(2):
        mix = left_mix if kind == 0 else right_mix
        for number in (2, 3, 4, 5):
            grow_copy(kind, number).wait_recv()

        def add_all(k, _):
            for j in range(SEC):
                part = pl.ds(j * HALF, HALF)
                total = (
                    outb[kind, 3, k, part].astype(F32)
                    + gath[kind, 1, k, part].astype(F32)
                    + gath[kind, 2, k, part].astype(F32)
                )
                work[j * channels + k, pl.ds(0, HALF)] = total * shrink
            part = pl.ds(SEC * HALF, 16)
            rows = (
                outb[kind, 3, k, part].astype(F32)
                + gath[kind, 1, k, part].astype(F32)
                + gath[kind, 2, k, part].astype(F32)
            )
            work[SEC * channels + k, pl.ds(0, 16)] = rows * shrink
            return 0

        lax.fori_loop(0, channels, add_all, 0)

        def blend(v, _):
            factors = [mix[k * channels + v] for k in range(channels)]
            rows = factors[0] * work[SEC * channels, pl.ds(0, 16)]
            for k in range(1, channels):
                rows = rows + factors[k] * work[SEC * channels + k, pl.ds(0, 16)]
            for j in range(SEC):
                upper = factors[0] * work[j * channels, pl.ds(0, HALF)]
                for k in range(1, channels):
                    upper = upper + factors[k] * work[j * channels + k, pl.ds(0, HALF)]
                row = jnp.sum(jnp.where(row16 == j, rows, 0.0), axis=0, keepdims=True)
                bound[kind, v, j] = unpack(upper.astype(BF16), row, bits)
            return 0

        lax.fori_loop(0, channels, blend, 0)
        store = pltpu.make_async_copy(
            bound.at[kind], left_out if kind == 0 else right_out, local_sem.at[kind]
        )
        store.start()
        stores.append(store)
    for store in stores:
        store.wait()
    for step in (1, 3, 2):
        wave_copy(step).wait_send()
    for kind in range(2):
        for number in range(6):
            grow_copy(kind, number).wait_send()


def body(
    left_boundary,
    right_boundary,
    psi_start,
    left_local,
    right_group,
    right_local,
    left_dims,
    right_dims,
    left_mix,
    right_mix,
):
    channels = left_boundary.shape[1]
    smem = pl.BlockSpec(memory_space=pltpu.SMEM)
    vmem = pl.BlockSpec(memory_space=pltpu.VMEM)
    hbm = pl.BlockSpec(memory_space=pl.ANY)
    table = pl.pallas_call(
        router,
        out_shape=jax.ShapeDtypeStruct((TABLE,), jnp.int32),
        in_specs=[smem] * 5,
        out_specs=smem,
        scratch_shapes=[pltpu.SMEM((16,), jnp.int32)],
        name="router",
    )(
        left_local.reshape(-1),
        right_group.reshape(-1),
        right_local.reshape(-1),
        left_dims.reshape(-1),
        right_dims.reshape(-1),
    )
    dma = pltpu.SemaphoreType.DMA
    env = (channels, SEC, N, N)
    wave, energy, left_grown, right_grown = pl.pallas_call(
        lambda *refs: kernel(channels, *refs),
        out_shape=(
            jax.ShapeDtypeStruct((RUN, N, N), BF16),
            jax.ShapeDtypeStruct((8, N), F32),
            jax.ShapeDtypeStruct(env, BF16),
            jax.ShapeDtypeStruct(env, BF16),
        ),
        in_specs=[smem, smem, smem, hbm, hbm, vmem],
        out_specs=(vmem, vmem, hbm, hbm),
        scratch_shapes=[
            pltpu.VMEM((2,) + env, BF16),
            pltpu.VMEM((2, SIDE * SEC, channels, N, N), BF16),
            pltpu.VMEM((2, SIDE, channels, PACK, N), BF16),
            pltpu.VMEM((2, SIDE, channels, PACK, N), BF16),
            pltpu.VMEM((max(4 * SLOTS, 8 * channels), N, N), F32),
            pltpu.VMEM((SLOTS, N, N), BF16),
            pltpu.VMEM((SLOTS, N, N), BF16),
            pltpu.VMEM((SLOTS, N, N), BF16),
            pltpu.VMEM((2, channels, N, N), BF16),
            pltpu.VMEM((3, SIDE * SIDE, 8, N), F32),
            pltpu.VMEM((3, 8, N), F32),
            dma((2,)),
            dma((6,)),
            dma((6,)),
            dma((2, channels)),
            dma((2, channels)),
            dma((2, 3, channels)),
            dma((2, 3, channels)),
            dma((3, SIDE * SIDE)),
            dma((3, SIDE * SIDE)),
            dma((2, 6)),
            dma((2, 6)),
        ],
        compiler_params=pltpu.CompilerParams(
            collective_id=0, has_side_effects=True, vmem_limit_bytes=62 * 2**20
        ),
        name="davidson",
    )(
        table,
        left_mix.reshape(-1),
        right_mix.reshape(-1),
        left_boundary[0],
        right_boundary[0],
        psi_start[0],
    )
    return wave[None], energy[0, :1], left_grown[None], right_grown[None]


def solution(mesh):
    return jax.shard_map(
        body,
        mesh=mesh,
        in_specs=(
            P("sect", None, "blk", None, None),
            P("sect", None, "blk", None, None),
            P("sect", "blk", None, None),
            P("sect", None),
            P("sect", None, None),
            P("sect", None),
            P("sect", None),
            P("sect", None),
            P(),
            P(),
        ),
        out_specs=(
            P("sect", "blk", None, None),
            P("sect"),
            P("sect", None, "blk", None, None),
            P("sect", None, "blk", None, None),
        ),
        check_vma=False,
    )
```

time: 1090 us -> 226 us (0.21); the launches traced: 1070 us -> 225 us
  blocking collectives: 579 us -> 0 us
  Pallas kernels: 0 us -> 210 us
  waiting for transfers between devices: 172 us -> 0 us
  matrix products: 125 us -> 0 us
  local copies, waits for them, and re-layouts: 134 us -> 10.8 us
  other arithmetic: 34.8 us -> 3.82 us
  starting transfers between devices: 17.9 us -> 0 us
    psum x7 -> x0, blocking collectives: 579 us -> none  [the longest x1 356 us: body(): start_sq = lax.psum(jnp.sum(start * start), 'blk')]
    pallas_call x0 -> x2, Pallas kernels: none -> 210 us  [the longest x1 203 us: body(): pl.pallas_call(lambda *refs: kernel(channels, *refs), out_shape=(jax.Shap...]
    all_to_all x2 -> x0, waiting for transfers between devices: 150 us -> none  [the longest x1 150 us: body(): lax.all_to_all(outgoing_terms, 'blk', split_axis=1, concat_axis=1, tiled=...]
    dot_general x9 -> x0, matrix products: 125 us -> none  [the longest x3 44.2 us: hamiltonian(): jnp.einsum('kexb,kedb->exd', inner, right_sel, preferred_element_type=jnp...]
    scatter x2 -> x0, local copies, waits for them, and re-layouts: 46.8 us -> none  [body(): outgoing_terms = jnp.zeros((channels, n_blocks * slot_count, block_size,...]
    gather x5 -> x0, local copies, waits for them, and re-layouts: 27.9 us -> none  [the longest x1 12.5 us: body(): right_sel = jnp.take(incoming, slot_mine, axis=1)]
    mul x1 -> x0, local copies, waits for them, and re-layouts: 27.2 us -> none  [body(): jnp.einsum('kead,ecd->keac', second, wave, preferred_element_type=jnp.flo...]
    ppermute x2 -> x0, waiting for transfers between devices: 21.9 us -> none  [from_behind(): return lax.ppermute(block, axis, route)]
  transfers between devices with their start and end apart: 4 -> 0, of which waited for: 2 -> 0; matrix products, arithmetic and copies ran while one was open for 8% -> 0% of each run, Pallas kernels for 0% -> 0%
where the time goes in v1:
time: 226 us; the launch traced here: 225 us
  Pallas kernels  210 us (93%)
  local copies, waits for them, and re-layouts  10.8 us (5%)
  other arithmetic  3.82 us (2%)
    pallas_call x1, Pallas kernels, body(): pl.pallas_call(lambda *refs: kernel(channels, *refs), out_shape=(jax.Shap...  203 us
    unnamed x5, local copies, waits for them, and re-layouts  6.86 us
    pallas_call x1, Pallas kernels, body(): pl.pallas_call(router, out_shape=jax.ShapeDtypeStruct((TABLE,), jnp.int32...  6.25 us

profile of v1, /device:TPU:64, one launch (start us, length us, event | category | flops | bytes accessed | tf_op | source)
XLA Modules:
  0.0 225.0 jit_solution(4858526444983744902)
XLA Ops:
  0.6 1.3 reduce.left_local
  1.9 1.3 reduce.1.right_group
  3.2 1.3 reduce.2.right_local
  4.5 6.2 %router.1.refs_0_ = s32[384]{0:T(512)} custom-call(s32[384]{0:T(512)} %reduce.left_local, s32[384]{0:T(512)} %reduce.1.right_group, s32[384]{0:T(512)} %reduce.2.right_local, s32[64]{0:T(128)} %bitcast.15, s32[64]{0:T(128)} %bitcast.16), custom_call_target="tpu_custom_call" | custom-call | tf_op jit(solution)/shard_map/router/pallas_call | solution.py:712
  10.7 1.4 reshape.34.refs_1_
  12.1 1.4 reshape.35.refs_2_
  13.5 203.5 %davidson.1 = (bf16[24,128,128]{2,1,0:T(8,128)(2,1)}, f32[8,128]{1,0:T(8,128)}, bf16[17,4,128,128]{3,2,1,0:T(8,128)(2,1)}, bf16[17,4,128,128]{3,2,1,0:T(8,128)(2,1)}) custom-call(s32[384]{0:T(512)} %router.1.refs_0_, f32[289]{0:T(512)} %reshape.34.refs_1_, f32[289]{0:T(512)} %reshape.35.refs_2_, bf16[17,4,128,128]{3,2,1,0:T(8,128)(2,1)} %bitcast.9, ...), custom_call_target="tpu_custom_call" | custom-call | tf_op jit(solution)/shard_map/davidson/pallas_call | solution.py:728
  217.0 1.2 slice.3
  218.2 2.1 copy.17
  220.2 0.0 copy-start
  220.2 3.4 %copy.18 = bf16[1,17,4,128,128]{4,3,2,1,0:T(8,128)(2,1)} copy(bf16[1,17,4,128,128]{4,3,2,1,0:T(8,128)(2,1)} %bitcast.12) | data formatting | bytes 4456448
  223.6 0.0 copy-done
  223.6 1.4 copy.19
Async XLA Ops:
  220.2 3.4 %copy-start = (bf16[17,4,128,128]{3,2,1,0:T(8,128)(2,1)S(1)}, bf16[17,4,128,128]{3,2,1,0:T(8,128)(2,1)}, u32[]{:S(2)}) copy-start(bf16[17,4,128,128]{3,2,1,0:T(8,128)(2,1)} %get-tuple-element.11) | copy-start | bytes 6684676

commit v2 on v1

--- a/solution.py
+++ b/solution.py
@@ -21,79 +21,75 @@
 RUN = 24
 PACK = SEC * HALF + 16
 UNROLL = 4
-LAG = 2
+AHEAD = 3
 
 SEND, SLOT_OF, LSEC, RSEC, LDIM, RDIM = 0, 32, 64, 96, 128, 160
 ORD_R, KEEP_R, LAST_R, LIVE_R = 192, 224, 256, 272
 ORD_L, KEEP_L, LAST_L, LIVE_L = 288, 320, 352, 368
-TABLE = 384
+SPARE = 384 - LSEC
+TABLE = 512
+
+
+def places(me, swap):
+    x, y = me // SIDE, me % SIDE
+    return x * (1 - swap) + y * swap, y * (1 - swap) + x * swap
+
+
+def device_at(u, w, swap):
+    return (u * SIDE + w) * (1 - swap) + (w * SIDE + u) * swap
 
 
 def router(left_local, right_group, right_local, left_dims, right_dims, table, count):
     me = lax.axis_index("blk")
-    my_x, my_y = me >> 2, me & 3
-
-    def clear(i, _):
+    swap = lax.axis_index("sect") & 1
+    my_u, my_w = places(me, swap)
+    for i in range(SLOTS):
         table[SEND + i] = 0
-        table[SLOT_OF + i] = 0
-        table[LSEC + i] = (i >> 3) * SEC
-        table[RSEC + i] = ((i & 7) >> 1) * SEC
+        table[LSEC + i] = (i // 8) * SEC
+        table[RSEC + i] = (i % 8 // 2) * SEC
         table[LDIM + i] = 0
         table[RDIM + i] = 0
-        return 0
-
-    lax.fori_loop(0, SLOTS, clear, 0)
 
     def zero_counts():
         for i in range(SIDE * SIDE):
             count[i] = 0
 
+    def split(group):
+        x, y = group >> 2, group & 3
+        return x * (1 - swap) + y * swap, y * (1 - swap) + x * swap
+
     zero_counts()
-
-    def own(e, _):
-        group = right_group[me * RUN + e]
+    for e in range(RUN):
+        group = right_group[0, me * RUN + e]
         rank = jnp.minimum(count[group], RANKS - 1)
         count[group] = rank + 1
-        slot = (group & 3) * 8 + (group >> 2) * 2 + rank
+        u, w = split(group)
+        slot = w * 8 + u * 2 + rank
         table[SLOT_OF + e] = slot
         table[SEND + slot] = e
-        return 0
-
-    lax.fori_loop(0, RUN, own, 0)
     for source in range(SIDE):
-        run = my_x * SIDE + source
+        run = device_at(my_u, source, swap)
         zero_counts()
-
-        def other(e, _):
+        for e in range(RUN):
             at = run * RUN + e
-            group = right_group[at]
+            group = right_group[0, at]
             rank = jnp.minimum(count[group], RANKS - 1)
             count[group] = rank + 1
-
-            @pl.when((group & 3) == my_y)
-            def _():
-                slot = source * 8 + (group >> 2) * 2 + rank
-                left, right = left_local[at], right_local[at]
-                table[LSEC + slot] = source * SEC + left
-                table[RSEC + slot] = (group >> 2) * SEC + right
-                table[LDIM + slot] = left_dims[run * SEC + left]
-                table[RDIM + slot] = right_dims[group * SEC + right]
-
-            return 0
-
-        lax.fori_loop(0, RUN, other, 0)
+            u, w = split(group)
+            slot = jnp.where(w == my_w, source * 8 + u * 2 + rank, SPARE)
+            left, right = left_local[0, at], right_local[0, at]
+            table[LSEC + slot] = source * SEC + left
+            table[RSEC + slot] = u * SEC + right
+            table[LDIM + slot] = left_dims[0, run * SEC + left]
+            table[RDIM + slot] = right_dims[0, group * SEC + right]
     for key, order, keep, last, live in (
         (LSEC, ORD_R, KEEP_R, LAST_R, LIVE_R),
         (RSEC, ORD_L, KEEP_L, LAST_L, LIVE_L),
     ):
         zero_counts()
-
-        def tally(s, _):
+        for s in range(SLOTS):
             sector = table[key + s]
             count[sector] = count[sector] + 1
-            return 0
-
-        lax.fori_loop(0, SLOTS, tally, 0)
         for g in range(SIDE):
             begin = jnp.int32(0)
             for j in range(SEC):
@@ -103,23 +99,17 @@
                 table[live + sector] = jnp.minimum(amount, 1)
                 begin = begin + amount
                 table[last + sector] = jnp.maximum(begin - 1, 0)
-
-        def place(s, _):
+        for s in range(SLOTS):
             sector = table[key + s]
             at = count[sector]
             count[sector] = at + 1
             table[order + at] = s
-            return 0
-
-        lax.fori_loop(0, SLOTS, place, 0)
-
-        def compare(p, _):
-            before = table[order + jnp.maximum(p - 1, 0)]
-            same = table[key + table[order + p]] == table[key + before]
-            table[keep + p] = jnp.where(jnp.logical_and((p & 7) != 0, same), 1, 0)
-            return 0
-
-        lax.fori_loop(0, SLOTS, compare, 0)
+        for g in range(SIDE):
+            before = jnp.int32(-1)
+            for p in range(g * 8, g * 8 + 8):
+                sector = table[key + table[order + p]]
+                table[keep + p] = jnp.where(sector == before, 1, 0)
+                before = sector
 
 
 def dot(a, b):
@@ -183,6 +173,7 @@
     red,
     mine,
     local_sem,
+    store_sem,
     psi_send,
     psi_recv,
     z_send,
@@ -197,15 +188,22 @@
     n_sect = lax.axis_size("sect")
     sect = lax.axis_index("sect")
     me = lax.axis_index("blk")
-    my_x, my_y = me // SIDE, me % SIDE
+    swap = sect % 2
+    my_u, my_w = places(me, swap)
     up, down = (sect + 1) % n_sect, (sect + n_sect - 1) % n_sect
-    half = channels // 2
-
-    def along_y(step):
-        return my_x * SIDE + (my_y + step) % SIDE
-
-    def along_x(step):
-        return ((my_x + step) % SIDE) * SIDE + my_y
+    deep = channels * HALF + 32
+    region = max(channels * PACK, SEC * deep)
+
+    def along(side, step):
+        if side == 0:
+            return device_at(my_u, (my_w + step) % SIDE, swap)
+        return device_at((my_u + step) % SIDE, my_w, swap)
+
+    def rows_of(group, k):
+        return pl.ds(pl.multiple_of(group * region + k * PACK, 16), PACK)
+
+    def sector_rows(place, j):
+        return pl.ds(pl.multiple_of(place * region + j * deep, 16), deep)
 
     barrier = pltpu.get_barrier_semaphore()
 
@@ -234,13 +232,13 @@
     pl.semaphore_wait(barrier, SIDE * SIDE + 1)
 
     def psi_copy(step):
-        to_y = (my_y + step) % SIDE
+        to_w = (my_w + step) % SIDE
         return pltpu.make_async_remote_copy(
-            src_ref=ret.at[pl.ds(to_y * 8, 8)],
-            dst_ref=vec.at[pl.ds(my_y * 8, 8)],
+            src_ref=ret.at[pl.ds(to_w * 8, 8)],
+            dst_ref=vec.at[pl.ds(my_w * 8, 8)],
             send_sem=psi_send.at[step - 1],
             recv_sem=psi_recv.at[step - 1],
-            device_id={"blk": along_y(step)},
+            device_id={"blk": along(0, step)},
             device_id_type=MESH,
         )
 
@@ -251,6 +249,7 @@
     below, left, low, high, diag = masks
     ones = [jnp.where(m, 1.0, 0.0).astype(BF16) for m in (below, left, low, high, diag)]
     bits = (ones[0], jnp.where(below, 0.0, 1.0).astype(BF16), ones[1], ones[2], ones[3], ones[4])
+    row32 = lax.broadcasted_iota(jnp.int32, (32, N), 0)
     row16 = lax.broadcasted_iota(jnp.int32, (16, N), 0)
     eye_packed = jnp.where(
         lax.broadcasted_iota(jnp.int32, (HALF, N), 0) == lax.broadcasted_iota(jnp.int32, (HALF, N), 1),
@@ -260,38 +259,33 @@
     eye_row = jnp.where(lax.broadcasted_iota(jnp.int32, (1, N), 1) >= HALF, 1.0, 0.0)
 
     def place(side):
-        return my_y if side == 0 else my_x
+        return my_w if side == 0 else my_u
 
     def z_copy(side, k):
         return pltpu.make_async_remote_copy(
-            src_ref=outb.at[side, 3, k],
-            dst_ref=gath.at[side, place(side), k],
+            src_ref=outb.at[side, rows_of(3, k)],
+            dst_ref=gath.at[side, rows_of(place(1 - side), k)],
             send_sem=z_send.at[side, k],
             recv_sem=z_recv.at[side, k],
             device_id={"sect": up if side == 0 else down},
             device_id_type=MESH,
         )
 
-    for load in loads:
-        load.wait()
-
-    def pack_bound(k, _):
+    def pack_bound(k):
         for side in range(2):
             edge = sect == (n_sect - 1 if side == 0 else 0)
             here = k == (0 if side == 0 else channels - 1)
+            one = jnp.where(here, 1.0, 0.0)
             rows = jnp.zeros((16, N), F32)
+            base = 3 * region + k * PACK
             for j in range(SEC):
                 upper, row = pack(bound[side, k, j].astype(F32), masks)
-                one = jnp.where(here, 1.0, 0.0)
                 upper = jnp.where(edge, eye_packed * one, upper)
                 row = jnp.where(edge, eye_row * one, row)
-                outb[side, 3, k, pl.ds(j * HALF, HALF)] = upper.astype(BF16)
+                outb[side, pl.ds(pl.multiple_of(base + j * HALF, 16), HALF)] = upper.astype(BF16)
                 rows = jnp.where(row16 == j, jnp.broadcast_to(row, (16, N)), rows)
-            outb[side, 3, k, pl.ds(SEC * HALF, 16)] = rows.astype(BF16)
+            outb[side, pl.ds(pl.multiple_of(base + SEC * HALF, 16), 16)] = rows.astype(BF16)
             z_copy(side, k).start()
-        return 0
-
-    lax.fori_loop(0, channels, pack_bound, 0)
 
     def ring_copy(side, which, k, back):
         at = place(side)
@@ -299,11 +293,11 @@
             at = (at + (1 if back else SIDE - 1)) % SIDE
         step = SIDE - 1 if back else 1
         return pltpu.make_async_remote_copy(
-            src_ref=gath.at[side, at, k],
-            dst_ref=gath.at[side, at, k],
+            src_ref=gath.at[side, rows_of(at, k)],
+            dst_ref=gath.at[side, rows_of(at, k)],
             send_sem=ring_send.at[side, which, k],
             recv_sem=ring_recv.at[side, which, k],
-            device_id={"blk": along_y(step) if side == 0 else along_x(step)},
+            device_id={"blk": along(side, step)},
             device_id_type=MESH,
         )
 
@@ -314,17 +308,25 @@
 
     X, HX, T, HT = 0, SLOTS, 2 * SLOTS, 3 * SLOTS
 
+    for load in loads:
+        load.wait()
+
     def gather_step(t, _):
         @pl.when(t < channels)
         def _():
+            pack_bound(t)
+
+        @pl.when(jnp.logical_and(t >= AHEAD, t < channels + AHEAD))
+        def _():
+            k = t - AHEAD
             for side in range(2):
-                z_copy(side, t).wait_recv()
-                ring_copy(side, 0, t, False).start()
-                ring_copy(side, 1, t, True).start()
-
-        @pl.when(jnp.logical_and(t >= 1, t < channels + 1))
+                z_copy(side, k).wait_recv()
+                ring_copy(side, 0, k, False).start()
+                ring_copy(side, 1, k, True).start()
+
+        @pl.when(jnp.logical_and(t >= 2 * AHEAD, t < channels + 2 * AHEAD))
         def _():
-            k = t - 1
+            k = t - 2 * AHEAD
             for side in range(2):
                 ring_copy(side, 0, k, False).wait_recv()
                 ring_copy(side, 1, k, True).wait_recv()
@@ -339,12 +341,12 @@
                 for side in range(2):
                     ring_copy(side, 2, k, True).start()
 
-        @pl.when(t == LAG)
+        @pl.when(t == 3 * AHEAD)
         def _():
             for step in (1, 3, 2):
                 psi_copy(step).wait_recv()
             for i in range(8):
-                vec[my_y * 8 + i] = ret[my_y * 8 + i]
+                vec[my_w * 8 + i] = ret[my_w * 8 + i]
 
             def start(i, _):
                 vec[i] = jnp.where(dims_mask(i), vec[i].astype(F32), 0.0).astype(BF16)
@@ -353,18 +355,19 @@
 
             lax.fori_loop(0, SLOTS, start, 0)
 
-        @pl.when(t >= LAG)
+        @pl.when(t >= 3 * AHEAD)
         def _():
-            k = t - LAG
+            k = t - 3 * AHEAD
             for side in range(2):
                 ring_copy(side, 2, k, False).wait_recv()
 
             def open_group(g, _):
+                base = g * region + k * PACK
                 for side in range(2):
-                    rows = gath[side, g, k, pl.ds(SEC * HALF, 16)].astype(F32)
+                    rows = gath[side, pl.ds(pl.multiple_of(base + SEC * HALF, 16), 16)].astype(F32)
                     for j in range(SEC):
                         row = jnp.sum(jnp.where(row16 == j, rows, 0.0), axis=0, keepdims=True)
-                        packed = gath[side, g, k, pl.ds(j * HALF, HALF)]
+                        packed = gath[side, pl.ds(pl.multiple_of(base + j * HALF, 16), HALF)]
                         cat[side, g * SEC + j, k] = unpack(packed, row, bits)
                 return 0
 
@@ -381,7 +384,7 @@
 
         return 0
 
-    lax.fori_loop(0, channels + LAG, gather_step, 0)
+    lax.fori_loop(0, channels + 3 * AHEAD, gather_step, 0)
 
     for step in (1, 3, 2):
         psi_copy(step).wait_send()
@@ -522,13 +525,13 @@
     lax.fori_loop(0, SLOTS, final_vector, 0)
 
     def wave_copy(step):
-        to_y = (my_y + step) % SIDE
+        to_w = (my_w + step) % SIDE
         return pltpu.make_async_remote_copy(
-            src_ref=vec.at[pl.ds(to_y * 8, 8)],
-            dst_ref=ret.at[pl.ds(my_y * 8, 8)],
+            src_ref=vec.at[pl.ds(to_w * 8, 8)],
+            dst_ref=ret.at[pl.ds(my_w * 8, 8)],
             send_sem=psi_send.at[step + 2],
             recv_sem=psi_recv.at[step + 2],
-            device_id={"blk": along_y(step)},
+            device_id={"blk": along(0, step)},
             device_id_type=MESH,
         )
 
@@ -557,80 +560,72 @@
 
         lax.fori_loop(0, 4, term, 0)
 
-        def close(k, _):
-            rows = jnp.zeros((16, N), F32)
+        def close(k, diagonals):
+            after = []
             for j in range(SEC):
                 spot = table[last + group * SEC + j]
+                upper, row = pack(work[spot * channels + k], masks)
+                at = pl.multiple_of(to * region + j * deep + k * HALF, 16)
                 has = table[live + group * SEC + j] > 0
-                upper, row = pack(work[spot * channels + k], masks)
-                outb[kind, to, k, pl.ds(j * HALF, HALF)] = jnp.where(has, upper, 0.0).astype(BF16)
-                row = jnp.where(has, row, 0.0)
-                rows = jnp.where(row16 == j, jnp.broadcast_to(row, (16, N)), rows)
-            outb[kind, to, k, pl.ds(SEC * HALF, 16)] = rows.astype(BF16)
-            return 0
-
-        lax.fori_loop(0, channels, close, 0)
-
-    first, second = pl.ds(0, half), pl.ds(half, channels - half)
-
-    def grow_copy(kind, number):
-        source, target, part, back = (
-            (0, 0, first, False),
-            (0, 0, second, True),
-            (1, 1, second, False),
-            (1, 1, first, False),
-            (2, 2, first, True),
-            (2, 2, second, True),
-        )[number]
-        step = SIDE - 1 if back else 1
+                outb[kind, pl.ds(at, HALF)] = jnp.where(has, upper, 0.0).astype(BF16)
+                after.append(jnp.where(row32 == k, jnp.broadcast_to(row, (32, N)), diagonals[j]))
+            return tuple(after)
+
+        diagonals = lax.fori_loop(0, channels, close, (jnp.zeros((32, N), F32),) * SEC)
+        for j in range(SEC):
+            has = table[live + group * SEC + j] > 0
+            at = to * region + j * deep + channels * HALF
+            outb[kind, pl.ds(at, 32)] = jnp.where(has, diagonals[j], 0.0).astype(BF16)
+
+    def grow_copy(kind, target, j):
+        back = target == 2 or (target == 0 and j >= 2)
         return pltpu.make_async_remote_copy(
-            src_ref=outb.at[kind, source, part],
-            dst_ref=gath.at[kind, target, part],
-            send_sem=grow_send.at[kind, number],
-            recv_sem=grow_recv.at[kind, number],
-            device_id={"blk": along_x(step) if kind == 0 else along_y(step)},
+            src_ref=outb.at[kind, sector_rows(target, j)],
+            dst_ref=gath.at[kind, sector_rows(target, j)],
+            send_sem=grow_send.at[kind, target, j],
+            recv_sem=grow_recv.at[kind, target, j],
+            device_id={"blk": along(1 - kind, SIDE - 1 if back else 1)},
             device_id_type=MESH,
         )
 
     def my_group(kind, step):
-        return ((my_x if kind == 0 else my_y) + step) % SIDE
-
-    for kind in range(2):
-        grow(kind, my_group(kind, 2), 0)
-        grow_copy(kind, 0).start()
-        grow_copy(kind, 1).start()
-    for kind in range(2):
-        grow(kind, my_group(kind, 1), 1)
-        grow_copy(kind, 2).start()
+        return ((my_u if kind == 0 else my_w) + step) % SIDE
+
     for step in (1, 3, 2):
         wave_copy(step).start()
     for kind in range(2):
+        grow(kind, my_group(kind, 2), 0)
+        for j in (0, 2, 1, 3):
+            grow_copy(kind, 0, j).start()
+    for kind in range(2):
+        grow(kind, my_group(kind, 1), 1)
+        for j in (2, 3):
+            grow_copy(kind, 1, j).start()
+    for kind in range(2):
         grow(kind, my_group(kind, SIDE - 1), 2)
-        grow_copy(kind, 4).start()
-    for kind in range(2):
-        grow_copy(kind, 0).wait_recv()
-
-        def add_first(k, _):
-            outb[kind, 1, k] = (outb[kind, 1, k].astype(F32) + gath[kind, 0, k].astype(F32)).astype(BF16)
-            return 0
-
-        lax.fori_loop(0, half, add_first, 0)
-        grow_copy(kind, 3).start()
-        grow_copy(kind, 1).wait_recv()
-
-        def add_second(k, _):
-            outb[kind, 2, k] = (outb[kind, 2, k].astype(F32) + gath[kind, 0, k].astype(F32)).astype(BF16)
-            return 0
-
-        lax.fori_loop(half, channels, add_second, 0)
-        grow_copy(kind, 5).start()
+        for j in (0, 1):
+            grow_copy(kind, 2, j).start()
+    for j in (0, 2, 1, 3):
+        target = 1 if j < 2 else 2
+        for kind in range(2):
+            grow_copy(kind, 0, j).wait_recv()
+
+            def add(i, _):
+                there = pl.ds(pl.multiple_of(target * region + j * deep + i * 32, 16), 32)
+                here = pl.ds(pl.multiple_of(j * deep + i * 32, 16), 32)
+                total = outb[kind, there].astype(F32) + gath[kind, here].astype(F32)
+                outb[kind, there] = total.astype(BF16)
+                return 0
+
+            lax.fori_loop(0, deep // 32, add, 0)
+            grow_copy(kind, target, j).start()
     for kind in range(2):
         grow(kind, my_group(kind, 0), 3)
 
     for step in (1, 3, 2):
         wave_copy(step).wait_recv()
     for i in range(8):
-        ret[my_y * 8 + i] = vec[my_y * 8 + i]
+        ret[my_w * 8 + i] = vec[my_w * 8 + i]
 
     def take(e, _):
         wave[e] = ret[table[SLOT_OF + e]]
@@ -639,58 +634,49 @@
     lax.fori_loop(0, RUN, take, 0)
 
     shrink = 1.0 / math.sqrt(N)
-    stores = []
+
+    def store(kind, j):
+        out = left_out if kind == 0 else right_out
+        return pltpu.make_async_copy(bound.at[kind, :, j], out.at[:, j], store_sem.at[kind, j])
+
+    for j, kind in [(j, kind) for j in (0, 2, 1, 3) for kind in range(2)]:
+        mix = left_mix if kind == 0 else right_mix
+        for target in (1, 2):
+            grow_copy(kind, target, j).wait_recv()
+
+        def total(at, size):
+            own, before, after = (
+                pl.ds(pl.multiple_of(spot * region + j * deep + at, 16), size) for spot in (3, 1, 2)
+            )
+            parts = outb[kind, own].astype(F32) + gath[kind, before].astype(F32)
+            return (parts + gath[kind, after].astype(F32)) * shrink
+
+        def add_all(k, _):
+            work[k, pl.ds(0, HALF)] = total(k * HALF, HALF)
+            return 0
+
+        lax.fori_loop(0, channels, add_all, 0)
+        work[channels, pl.ds(0, 32)] = total(channels * HALF, 32)
+
+        def blend(v, _):
+            factors = [mix[k, v] for k in range(channels)]
+            row = factors[0] * work[channels, pl.ds(0, 1)]
+            upper = factors[0] * work[0, pl.ds(0, HALF)]
+            for k in range(1, channels):
+                row = row + factors[k] * work[channels, pl.ds(k, 1)]
+                upper = upper + factors[k] * work[k, pl.ds(0, HALF)]
+            bound[kind, v, j] = unpack(upper.astype(BF16), row, bits)
+            return 0
+
+        lax.fori_loop(0, channels, blend, 0)
+        store(kind, j).start()
     for kind in range(2):
-        mix = left_mix if kind == 0 else right_mix
-        for number in (2, 3, 4, 5):
-            grow_copy(kind, number).wait_recv()
-
-        def add_all(k, _):
-            for j in range(SEC):
-                part = pl.ds(j * HALF, HALF)
-                total = (
-                    outb[kind, 3, k, part].astype(F32)
-                    + gath[kind, 1, k, part].astype(F32)
-                    + gath[kind, 2, k, part].astype(F32)
-                )
-                work[j * channels + k, pl.ds(0, HALF)] = total * shrink
-            part = pl.ds(SEC * HALF, 16)
-            rows = (
-                outb[kind, 3, k, part].astype(F32)
-                + gath[kind, 1, k, part].astype(F32)
-                + gath[kind, 2, k, part].astype(F32)
-            )
-            work[SEC * channels + k, pl.ds(0, 16)] = rows * shrink
-            return 0
-
-        lax.fori_loop(0, channels, add_all, 0)
-
-        def blend(v, _):
-            factors = [mix[k * channels + v] for k in range(channels)]
-            rows = factors[0] * work[SEC * channels, pl.ds(0, 16)]
-            for k in range(1, channels):
-                rows = rows + factors[k] * work[SEC * channels + k, pl.ds(0, 16)]
-            for j in range(SEC):
-                upper = factors[0] * work[j * channels, pl.ds(0, HALF)]
-                for k in range(1, channels):
-                    upper = upper + factors[k] * work[j * channels + k, pl.ds(0, HALF)]
-                row = jnp.sum(jnp.where(row16 == j, rows, 0.0), axis=0, keepdims=True)
-                bound[kind, v, j] = unpack(upper.astype(BF16), row, bits)
-            return 0
-
-        lax.fori_loop(0, channels, blend, 0)
-        store = pltpu.make_async_copy(
-            bound.at[kind], left_out if kind == 0 else right_out, local_sem.at[kind]
-        )
-        store.start()
-        stores.append(store)
-    for store in stores:
-        store.wait()
+        for j in range(SEC):
+            store(kind, j).wait()
+            for target in range(3):
+                grow_copy(kind, target, j).wait_send()
     for step in (1, 3, 2):
         wave_copy(step).wait_send()
-    for kind in range(2):
-        for number in range(6):
-            grow_copy(kind, number).wait_send()
 
 
 def body(
@@ -717,14 +703,15 @@
         scratch_shapes=[pltpu.SMEM((16,), jnp.int32)],
         name="router",
     )(
-        left_local.reshape(-1),
-        right_group.reshape(-1),
-        right_local.reshape(-1),
-        left_dims.reshape(-1),
-        right_dims.reshape(-1),
+        left_local,
+        right_group[:, :, 0],
+        right_local,
+        left_dims,
+        right_dims,
     )
     dma = pltpu.SemaphoreType.DMA
     env = (channels, SEC, N, N)
+    region = max(channels * PACK, SEC * (channels * HALF + 32))
     wave, energy, left_grown, right_grown = pl.pallas_call(
         lambda *refs: kernel(channels, *refs),
         out_shape=(
@@ -738,8 +725,8 @@
         scratch_shapes=[
             pltpu.VMEM((2,) + env, BF16),
             pltpu.VMEM((2, SIDE * SEC, channels, N, N), BF16),
-            pltpu.VMEM((2, SIDE, channels, PACK, N), BF16),
-            pltpu.VMEM((2, SIDE, channels, PACK, N), BF16),
+            pltpu.VMEM((2, SIDE * region, N), BF16),
+            pltpu.VMEM((2, SIDE * region, N), BF16),
             pltpu.VMEM((max(4 * SLOTS, 8 * channels), N, N), F32),
             pltpu.VMEM((SLOTS, N, N), BF16),
             pltpu.VMEM((SLOTS, N, N), BF16),
@@ -748,6 +735,7 @@
             pltpu.VMEM((3, SIDE * SIDE, 8, N), F32),
             pltpu.VMEM((3, 8, N), F32),
             dma((2,)),
+            dma((2, SEC)),
             dma((6,)),
             dma((6,)),
             dma((2, channels)),
@@ -756,8 +744,8 @@
             dma((2, 3, channels)),
             dma((3, SIDE * SIDE)),
             dma((3, SIDE * SIDE)),
-            dma((2, 6)),
-            dma((2, 6)),
+            dma((2, 3, SEC)),
+            dma((2, 3, SEC)),
         ],
         compiler_params=pltpu.CompilerParams(
             collective_id=0, has_side_effects=True, vmem_limit_bytes=62 * 2**20
@@ -765,8 +753,8 @@
         name="davidson",
     )(
         table,
-        left_mix.reshape(-1),
-        right_mix.reshape(-1),
+        left_mix,
+        right_mix,
         left_boundary[0],
         right_boundary[0],
         psi_start[0],

time: 226 us -> 214 us (0.947)
  Pallas kernels: 210 us -> 203 us
  other arithmetic: 3.82 us -> 0 us
  local copies, waits for them, and re-layouts: 10.8 us -> 8.04 us
    pallas_call x1, Pallas kernels: 203 us -> 199 us  [body(): pl.pallas_call(lambda *refs: kernel(channels, *refs), out_shape=(jax.Shap...]
    unnamed x3 -> x0, other arithmetic: 3.82 us -> none
    reshape x2 -> x0, local copies, waits for them, and re-layouts: 2.75 us -> none  [the longest x1 1.38 us: body(): left_mix.reshape(-1)]
    pallas_call x1, Pallas kernels: 6.25 us -> 3.78 us  [body(): pl.pallas_call(router, out_shape=jax.ShapeDtypeStruct((TABLE,), jnp.int32...]
where the time goes in v2:
time: 214 us; the launch traced here: 212 us
  Pallas kernels  203 us (95%)
  local copies, waits for them, and re-layouts  8.04 us (4%)
    pallas_call x1, Pallas kernels, body(): pl.pallas_call(lambda *refs: kernel(channels, *refs), out_shape=(jax.Shap...  199 us
    unnamed x5, local copies, waits for them, and re-layouts  6.86 us

profile of v2, /device:TPU:64, one launch (start us, length us, event | category | flops | bytes accessed | tf_op | source)
XLA Modules:
  0.0 211.5 jit_solution(13742571840716109290)
XLA Ops:
  0.6 3.8 %router.1.refs_0_ = s32[512]{0:T(512)} custom-call(s32[1,384]{1,0:T(1,128)} %left_local.1, s32[1,384]{1,0:T(1,128)} %bitcast.14, s32[1,384]{1,0:T(1,128)} %right_local.1, s32[1,64]{1,0:T(1,128)} %left_dims.1, s32[1,64]{1,0:T(1,128)} %right_dims.1), custom_call_target="tpu_custom_call" | custom-call | tf_op jit(solution)/shard_map/router/pallas_call | solution.py:698
  4.4 199.0 %davidson.1 = (bf16[24,128,128]{2,1,0:T(8,128)(2,1)}, f32[8,128]{1,0:T(8,128)}, bf16[17,4,128,128]{3,2,1,0:T(8,128)(2,1)}, bf16[17,4,128,128]{3,2,1,0:T(8,128)(2,1)}) custom-call(s32[512]{0:T(512)} %router.1.refs_0_, f32[17,17]{1,0:T(8,128)} %refs_1_.1, f32[17,17]{1,0:T(8,128)} %refs_2_.1, bf16[17,4,128,128]{3,2,1,0:T(8,128)(2,1)} %bitcast.8, ...), custom_call_target="tpu_custom_call" | custom-call | tf_op jit(solution)/shard_map/davidson/pallas_call | solution.py:715
  203.5 1.2 slice.3
  204.7 2.1 copy.17
  206.7 0.0 copy-start
  206.7 3.4 %copy.18 = bf16[1,17,4,128,128]{4,3,2,1,0:T(8,128)(2,1)} copy(bf16[1,17,4,128,128]{4,3,2,1,0:T(8,128)(2,1)} %bitcast.11) | data formatting | bytes 4456448
  210.2 0.0 copy-done
  210.2 1.4 copy.19
Async XLA Ops:
  206.7 3.4 %copy-start = (bf16[17,4,128,128]{3,2,1,0:T(8,128)(2,1)S(1)}, bf16[17,4,128,128]{3,2,1,0:T(8,128)(2,1)}, u32[]{:S(2)}) copy-start(bf16[17,4,128,128]{3,2,1,0:T(8,128)(2,1)} %get-tuple-element.11) | copy-start | bytes 6684676

commit v3 on v2

--- a/solution.py
+++ b/solution.py
@@ -21,6 +21,7 @@
 RUN = 24
 PACK = SEC * HALF + 16
 UNROLL = 4
+TERMS = 4
 AHEAD = 3
 
 SEND, SLOT_OF, LSEC, RSEC, LDIM, RDIM = 0, 32, 64, 96, 128, 160
@@ -168,6 +169,8 @@
     work,
     vec,
     vect,
+    vecr,
+    vectr,
     ret,
     stack,
     red,
@@ -247,6 +250,7 @@
 
     masks = triangle_masks()
     below, left, low, high, diag = masks
+    diag_low = lax.broadcasted_iota(jnp.int32, (HALF, N), 0) == lax.broadcasted_iota(jnp.int32, (HALF, N), 1)
     ones = [jnp.where(m, 1.0, 0.0).astype(BF16) for m in (below, left, low, high, diag)]
     bits = (ones[0], jnp.where(below, 0.0, 1.0).astype(BF16), ones[1], ones[2], ones[3], ones[4])
     row32 = lax.broadcasted_iota(jnp.int32, (32, N), 0)
@@ -311,6 +315,16 @@
     for load in loads:
         load.wait()
 
+    def beside(side, sector, lo=0, hi=channels):
+        return jnp.concatenate([cat[side, sector, k] for k in range(lo, hi)], axis=1)
+
+    def product(blocks, slots, lo=0, hi=channels):
+        inner = []
+        for block, s in zip(blocks, slots):
+            z = dot(block, beside(1, table[RSEC + s], lo, hi)).astype(BF16)
+            inner.append(jnp.concatenate([z[:, k * N : (k + 1) * N] for k in range(hi - lo)], axis=0))
+        return [dot(beside(0, table[LSEC + s], lo, hi), z) for s, z in zip(slots, inner)]
+
     def gather_step(t, _):
         @pl.when(t < channels)
         def _():
@@ -350,7 +364,6 @@
 
             def start(i, _):
                 vec[i] = jnp.where(dims_mask(i), vec[i].astype(F32), 0.0).astype(BF16)
-                work[HX + i] = jnp.zeros((N, N), F32)
                 return 0
 
             lax.fori_loop(0, SLOTS, start, 0)
@@ -373,14 +386,19 @@
 
             lax.fori_loop(0, SIDE, open_group, 0)
 
-            def apply(i, _):
-                slots = [i * UNROLL + u for u in range(UNROLL)]
-                inner = [dot(vec[s], cat[1, table[RSEC + s], k]).astype(BF16) for s in slots]
-                for s, z in zip(slots, inner):
-                    work[HX + s] += dot(cat[0, table[LSEC + s], k], z)
-                return 0
-
-            lax.fori_loop(0, SLOTS // UNROLL, apply, 0)
+            bounds = [4 * n for n in range(max(channels // 4, 1))] + [channels]
+            for lo, hi in zip(bounds[:-1], bounds[1:]):
+
+                @pl.when(k == hi - 1)
+                def _():
+                    def apply(i, _):
+                        slots = [i * UNROLL + u for u in range(UNROLL)]
+                        images = product([vec[s] for s in slots], slots, lo, hi)
+                        for s, image in zip(slots, images):
+                            work[HX + s] = image if lo == 0 else work[HX + s] + image
+                        return 0
+
+                    lax.fori_loop(0, SLOTS // UNROLL, apply, 0)
 
         return 0
 
@@ -448,40 +466,29 @@
     hxhx = hh / (norm * norm)
     b = jnp.sqrt(jnp.maximum(hxhx - 2.0 * a * a + a * a * xx, 0.0) + EPSILON)
 
-    def first_residual(s, _):
-        x = vec[s].astype(F32) / norm
-        hx = work[HX + s] / norm
-        t = (hx - a * x) / b
-        work[X + s] = x
-        work[HX + s] = hx
-        work[T + s] = t
-        vec[s] = t.astype(BF16)
-        return 0
-
-    lax.fori_loop(0, SLOTS, first_residual, 0)
-
-    def beside(side, sector):
-        return jnp.concatenate([cat[side, sector, k] for k in range(channels)], axis=1)
-
-    def hamiltonian(i, _):
+    per_norm, per_b = 1.0 / norm, 1.0 / b
+
+    def first_correction(i, sums):
         slots = [i * UNROLL + u for u in range(UNROLL)]
-        inner = []
+        blocks = []
         for s in slots:
-            z = dot(vec[s], beside(1, table[RSEC + s])).astype(BF16)
-            inner.append(jnp.concatenate([z[:, k * N : (k + 1) * N] for k in range(channels)], axis=0))
-        for s, z in zip(slots, inner):
-            work[HT + s] = jnp.where(dims_mask(s), dot(beside(0, table[LSEC + s]), z), 0.0)
-        return 0
-
-    lax.fori_loop(0, SLOTS // UNROLL, hamiltonian, 0)
-
-    def second_sums(s, sums):
-        x, hx, t, ht = work[X + s], work[HX + s], work[T + s], work[HT + s]
-        terms = (x * t, t * t, x * ht, t * hx, t * ht, hx * ht, ht * ht)
-        return tuple(old + fold(term) for old, term in zip(sums, terms))
+            x = vec[s].astype(F32) * per_norm
+            hx = work[HX + s] * per_norm
+            t = (hx - a * x) * per_b
+            work[X + s] = x
+            work[HX + s] = hx
+            work[T + s] = t
+            blocks.append(t.astype(BF16))
+        for s, image in zip(slots, product(blocks, slots)):
+            ht = jnp.where(dims_mask(s), image, 0.0)
+            work[HT + s] = ht
+            x, hx, t = work[X + s], work[HX + s], work[T + s]
+            terms = (x * t, t * t, x * ht, t * hx, t * ht, hx * ht, ht * ht)
+            sums = tuple(old + fold(term) for old, term in zip(sums, terms))
+        return sums
 
     xt, tt, xht, thx, c, hxht, htht = exchange(
-        1, lax.fori_loop(0, SLOTS, second_sums, (zero8,) * 7)
+        1, lax.fori_loop(0, SLOTS // UNROLL, first_correction, (zero8,) * 7)
     )
 
     def ritz(a, b, c):
@@ -496,30 +503,34 @@
     hxhx2 = p * p * hxhx + 2.0 * p * q * hxht + q * q * htht
     b2 = jnp.sqrt(jnp.maximum(hxhx2 - 2.0 * a2 * a2 + a2 * a2 * xx2, 0.0) + EPSILON)
 
-    def second_residual(s, _):
-        x = p * work[X + s] + q * work[T + s]
-        hx = p * work[HX + s] + q * work[HT + s]
-        t = (hx - a2 * x) / b2
-        work[X + s] = x
-        work[T + s] = t
-        vec[s] = t.astype(BF16)
-        return 0
-
-    lax.fori_loop(0, SLOTS, second_residual, 0)
-    lax.fori_loop(0, SLOTS // UNROLL, hamiltonian, 0)
-
-    def third_sums(s, total):
-        return total + fold(work[T + s] * work[HT + s])
-
-    (c2,) = exchange(2, [lax.fori_loop(0, SLOTS, third_sums, zero8)])
+    per_b2 = 1.0 / b2
+
+    def second_correction(i, total):
+        slots = [i * UNROLL + u for u in range(UNROLL)]
+        blocks = []
+        for s in slots:
+            x = p * work[X + s] + q * work[T + s]
+            hx = p * work[HX + s] + q * work[HT + s]
+            t = (hx - a2 * x) * per_b2
+            work[X + s] = x
+            work[T + s] = t
+            blocks.append(t.astype(BF16))
+        for s, image in zip(slots, product(blocks, slots)):
+            total = total + fold(work[T + s] * jnp.where(dims_mask(s), image, 0.0))
+        return total
+
+    (c2,) = exchange(2, [lax.fori_loop(0, SLOTS // UNROLL, second_correction, zero8)])
     value, p2, q2 = ritz(a2, b2, c2)
     energy[...] = jnp.broadcast_to(value, (8, N))
     scale = N * math.sqrt(RUN * SIDE * SIDE)
 
     def final_vector(s, _):
         w = ((p2 * work[X + s] + q2 * work[T + s]) * scale).astype(BF16)
+        turned = w.T
         vec[s] = w
-        vect[s] = w.T
+        vect[s] = turned
+        vecr[s] = pltpu.roll(w.astype(F32), HALF, 1).astype(BF16)
+        vectr[s] = pltpu.roll(turned.astype(F32), HALF, 1).astype(BF16)
         return 0
 
     lax.fori_loop(0, SLOTS, final_vector, 0)
@@ -540,31 +551,47 @@
             (ORD_L, KEEP_L, LAST_L, LIVE_L) if kind == 0 else (ORD_R, KEEP_R, LAST_R, LIVE_R)
         )
         outer, sector_at = (vect, LSEC) if kind == 0 else (vec, RSEC)
-        closing = vec if kind == 0 else vect
+        closing, closing_rolled = (vec, vecr) if kind == 0 else (vect, vectr)
+        nothing = jnp.zeros((N, N), BF16)
 
         def term(i, _):
-            spots = [i * 2 + u for u in range(2)]
-            for u, spot in enumerate(spots):
-                slot = table[order + group * 8 + spot]
+            spots = [i * TERMS + u for u in range(TERMS)]
+            slots = [table[order + group * 8 + spot] for spot in spots]
+            for u, slot in enumerate(slots):
                 z = dot(outer[slot], beside(kind, table[sector_at + slot])).astype(BF16)
                 for k in range(channels):
-                    stack[u, k] = z[:, k * N : (k + 1) * N]
-            for u, spot in enumerate(spots):
-                slot = table[order + group * 8 + spot]
+                    part = z[:, k * N : (k + 1) * N]
+                    stack[u, pl.ds(k * HALF, HALF), pl.ds(0, N)] = part[:HALF]
+                    stack[u, pl.ds(k * HALF, HALF), pl.ds(N, N)] = part[HALF:]
+            for u, (spot, slot) in enumerate(zip(spots, slots)):
+                square = jnp.concatenate(
+                    [
+                        jnp.concatenate([closing[slot], nothing], axis=1),
+                        jnp.concatenate([nothing, closing_rolled[slot]], axis=1),
+                    ],
+                    axis=0,
+                )
+                both = dot(stack[u], square)
                 stay = table[keep + group * 8 + spot] > 0
-                right = closing[slot]
                 for k in range(channels):
-                    before = work[jnp.maximum(spot - 1, 0) * channels + k]
-                    work[spot * channels + k] = dot(stack[u, k], right) + jnp.where(stay, before, 0.0)
+                    rows = both[k * HALF : (k + 1) * HALF]
+                    upper = jnp.where(below, rows[:, N:], rows[:, :N])
+                    trace = jnp.where(diag_low, rows[:, N:], 0.0)
+                    trace = jnp.sum(trace.reshape(HALF // 8, 8, N), axis=0)
+                    before = jnp.maximum(spot - 1, 0) * channels + k
+                    now = spot * channels + k
+                    work[now, pl.ds(0, HALF)] = upper + jnp.where(stay, work[before, pl.ds(0, HALF)], 0.0)
+                    work[now, pl.ds(HALF, 8)] = trace + jnp.where(stay, work[before, pl.ds(HALF, 8)], 0.0)
             return 0
 
-        lax.fori_loop(0, 4, term, 0)
+        lax.fori_loop(0, 8 // TERMS, term, 0)
 
         def close(k, diagonals):
             after = []
             for j in range(SEC):
                 spot = table[last + group * SEC + j]
-                upper, row = pack(work[spot * channels + k], masks)
+                upper = work[spot * channels + k, pl.ds(0, HALF)]
+                row = jnp.sum(work[spot * channels + k, pl.ds(HALF, 8)], axis=0, keepdims=True)
                 at = pl.multiple_of(to * region + j * deep + k * HALF, 16)
                 has = table[live + group * SEC + j] > 0
                 outb[kind, pl.ds(at, HALF)] = jnp.where(has, upper, 0.0).astype(BF16)
@@ -656,7 +683,7 @@
             return 0
 
         lax.fori_loop(0, channels, add_all, 0)
-        work[channels, pl.ds(0, 32)] = total(channels * HALF, 32)
+        work[channels, pl.ds(0, 32)] = pltpu.roll(total(channels * HALF, 32), HALF, 1)
 
         def blend(v, _):
             factors = [mix[k, v] for k in range(channels)]
@@ -731,7 +758,9 @@
             pltpu.VMEM((SLOTS, N, N), BF16),
             pltpu.VMEM((SLOTS, N, N), BF16),
             pltpu.VMEM((SLOTS, N, N), BF16),
-            pltpu.VMEM((2, channels, N, N), BF16),
+            pltpu.VMEM((SLOTS, N, N), BF16),
+            pltpu.VMEM((SLOTS, N, N), BF16),
+            pltpu.VMEM((TERMS, channels * HALF, 2 * N), BF16),
             pltpu.VMEM((3, SIDE * SIDE, 8, N), F32),
             pltpu.VMEM((3, 8, N), F32),
             dma((2,)),

time: 214 us -> 182 us (0.85); the launches traced: 212 us -> 182 us
  Pallas kernels: 203 us -> 174 us
    pallas_call x1, Pallas kernels: 199 us -> 170 us  [body(): pl.pallas_call(lambda *refs: kernel(channels, *refs), out_shape=(jax.Shap...]
where the time goes in v3:
time: 182 us
  Pallas kernels  174 us (96%)
  local copies, waits for them, and re-layouts  8.04 us (4%)
    pallas_call x1, Pallas kernels, body(): pl.pallas_call(lambda *refs: kernel(channels, *refs), out_shape=(jax.Shap...  170 us
    unnamed x5, local copies, waits for them, and re-layouts  6.86 us
    pallas_call x1, Pallas kernels, body(): pl.pallas_call(router, out_shape=jax.ShapeDtypeStruct((TABLE,), jnp.int32...  3.78 us

profile of v3, /device:TPU:64, one launch (start us, length us, event | category | flops | bytes accessed | tf_op | source)
XLA Modules:
  0.0 182.2 jit_solution(756083727261056661)
XLA Ops:
  0.6 3.8 %router.1.refs_0_ = s32[512]{0:T(512)} custom-call(s32[1,384]{1,0:T(1,128)} %left_local.1, s32[1,384]{1,0:T(1,128)} %bitcast.14, s32[1,384]{1,0:T(1,128)} %right_local.1, s32[1,64]{1,0:T(1,128)} %left_dims.1, s32[1,64]{1,0:T(1,128)} %right_dims.1), custom_call_target="tpu_custom_call" | custom-call | tf_op jit(solution)/shard_map/router/pallas_call | solution.py:725
  4.4 169.7 %davidson.1 = (bf16[24,128,128]{2,1,0:T(8,128)(2,1)}, f32[8,128]{1,0:T(8,128)}, bf16[17,4,128,128]{3,2,1,0:T(8,128)(2,1)}, bf16[17,4,128,128]{3,2,1,0:T(8,128)(2,1)}) custom-call(s32[512]{0:T(512)} %router.1.refs_0_, f32[17,17]{1,0:T(8,128)} %refs_1_.1, f32[17,17]{1,0:T(8,128)} %refs_2_.1, bf16[17,4,128,128]{3,2,1,0:T(8,128)(2,1)} %bitcast.8, ...), custom_call_target="tpu_custom_call" | custom-call | tf_op jit(solution)/shard_map/davidson/pallas_call | solution.py:742
  174.2 1.2 slice.3
  175.3 2.1 %copy.17 = bf16[1,24,128,128]{3,2,1,0:T(8,128)(2,1)} copy(bf16[1,24,128,128]{3,2,1,0:T(8,128)(2,1)} %bitcast.13) | data formatting | bytes 1572864
  177.4 0.0 copy-start
  177.4 3.4 %copy.18 = bf16[1,17,4,128,128]{4,3,2,1,0:T(8,128)(2,1)} copy(bf16[1,17,4,128,128]{4,3,2,1,0:T(8,128)(2,1)} %bitcast.11) | data formatting | bytes 4456448
  180.8 0.0 copy-done
  180.8 1.4 copy.19
Async XLA Ops:
  177.4 3.4 %copy-start = (bf16[17,4,128,128]{3,2,1,0:T(8,128)(2,1)S(1)}, bf16[17,4,128,128]{3,2,1,0:T(8,128)(2,1)}, u32[]{:S(2)}) copy-start(bf16[17,4,128,128]{3,2,1,0:T(8,128)(2,1)} %get-tuple-element.11) | copy-start | bytes 6684676

commit v4 on v3

--- a/solution.py
+++ b/solution.py
@@ -22,7 +22,7 @@
 PACK = SEC * HALF + 16
 UNROLL = 4
 TERMS = 4
-AHEAD = 3
+RING, HAND, OPEN = 3, 7, 10
 
 SEND, SLOT_OF, LSEC, RSEC, LDIM, RDIM = 0, 32, 64, 96, 128, 160
 ORD_R, KEEP_R, LAST_R, LIVE_R = 192, 224, 256, 272
@@ -173,6 +173,7 @@
     vectr,
     ret,
     stack,
+    spread,
     red,
     mine,
     local_sem,
@@ -262,6 +263,19 @@
     )
     eye_row = jnp.where(lax.broadcasted_iota(jnp.int32, (1, N), 1) >= HALF, 1.0, 0.0)
 
+    lane = lax.broadcasted_iota(jnp.int32, (8, 2 * N), 1) - lax.broadcasted_iota(jnp.int32, (8, 2 * N), 0)
+    spread[...] = jnp.zeros_like(spread)
+
+    def spread_mix(v, _):
+        for kind, mix in enumerate((left_mix, right_mix)):
+            rows = jnp.zeros((8, 2 * N), F32)
+            for k in range(channels):
+                rows = jnp.where(lane == 8 * k, mix[k, v], rows)
+            spread[kind, pl.ds(pl.multiple_of(v * 8, 8), 8)] = rows
+        return 0
+
+    lax.fori_loop(0, channels, spread_mix, 0)
+
     def place(side):
         return my_w if side == 0 else my_u
 
@@ -330,17 +344,17 @@
         def _():
             pack_bound(t)
 
-        @pl.when(jnp.logical_and(t >= AHEAD, t < channels + AHEAD))
+        @pl.when(jnp.logical_and(t >= RING, t < channels + RING))
         def _():
-            k = t - AHEAD
+            k = t - RING
             for side in range(2):
                 z_copy(side, k).wait_recv()
                 ring_copy(side, 0, k, False).start()
                 ring_copy(side, 1, k, True).start()
 
-        @pl.when(jnp.logical_and(t >= 2 * AHEAD, t < channels + 2 * AHEAD))
+        @pl.when(jnp.logical_and(t >= HAND, t < channels + HAND))
         def _():
-            k = t - 2 * AHEAD
+            k = t - HAND
             for side in range(2):
                 ring_copy(side, 0, k, False).wait_recv()
                 ring_copy(side, 1, k, True).wait_recv()
@@ -355,7 +369,7 @@
                 for side in range(2):
                     ring_copy(side, 2, k, True).start()
 
-        @pl.when(t == 3 * AHEAD)
+        @pl.when(t == OPEN)
         def _():
             for step in (1, 3, 2):
                 psi_copy(step).wait_recv()
@@ -368,9 +382,9 @@
 
             lax.fori_loop(0, SLOTS, start, 0)
 
-        @pl.when(t >= 3 * AHEAD)
+        @pl.when(t >= OPEN)
         def _():
-            k = t - 3 * AHEAD
+            k = t - OPEN
             for side in range(2):
                 ring_copy(side, 2, k, False).wait_recv()
 
@@ -386,7 +400,7 @@
 
             lax.fori_loop(0, SIDE, open_group, 0)
 
-            bounds = [4 * n for n in range(max(channels // 4, 1))] + [channels]
+            bounds = list(range(0, channels, 5)) + [channels]
             for lo, hi in zip(bounds[:-1], bounds[1:]):
 
                 @pl.when(k == hi - 1)
@@ -402,7 +416,7 @@
 
         return 0
 
-    lax.fori_loop(0, channels + 3 * AHEAD, gather_step, 0)
+    lax.fori_loop(0, channels + OPEN, gather_step, 0)
 
     for step in (1, 3, 2):
         psi_copy(step).wait_send()
@@ -667,7 +681,6 @@
         return pltpu.make_async_copy(bound.at[kind, :, j], out.at[:, j], store_sem.at[kind, j])
 
     for j, kind in [(j, kind) for j in (0, 2, 1, 3) for kind in range(2)]:
-        mix = left_mix if kind == 0 else right_mix
         for target in (1, 2):
             grow_copy(kind, target, j).wait_recv()
 
@@ -678,24 +691,40 @@
             parts = outb[kind, own].astype(F32) + gath[kind, before].astype(F32)
             return (parts + gath[kind, after].astype(F32)) * shrink
 
-        def add_all(k, _):
+        diagonals = pltpu.roll(total(channels * HALF, 32), HALF, 1)
+        for k in range(channels):
             work[k, pl.ds(0, HALF)] = total(k * HALF, HALF)
+            work[k, pl.ds(HALF, 8)] = jnp.broadcast_to(diagonals[k : k + 1], (8, N))
+
+        factor = spread[kind]
+        high_part = factor.astype(BF16)
+        low_part = (factor - high_part.astype(F32)).astype(BF16)
+
+        def eight(r):
+            rows = [work[k, pl.ds(r * 8, 8)] for k in range(channels)]
+            rows.append(jnp.zeros((2 * N - 8 * channels, N), F32))
+            return jnp.concatenate(rows, axis=0).astype(BF16)
+
+        for start in range(0, 9, 2):
+            count = min(2, 9 - start)
+            rows = jnp.concatenate([eight(start + n) for n in range(count)], axis=1)
+            mixed = dot(high_part, rows) + dot(low_part, rows)
+            for v in range(channels):
+                for n in range(count):
+                    work[32 + v, pl.ds((start + n) * 8, 8)] = mixed[v * 8 : v * 8 + 8, n * N : n * N + N]
+
+        def grown(v):
+            upper = work[32 + v, pl.ds(0, HALF)].astype(BF16)
+            bound[kind, v, j] = unpack(upper, work[32 + v, pl.ds(HALF, 1)], bits)
+
+        def several(i, _):
+            for n in range(4):
+                grown(i * 4 + n)
             return 0
 
-        lax.fori_loop(0, channels, add_all, 0)
-        work[channels, pl.ds(0, 32)] = pltpu.roll(total(channels * HALF, 32), HALF, 1)
-
-        def blend(v, _):
-            factors = [mix[k, v] for k in range(channels)]
-            row = factors[0] * work[channels, pl.ds(0, 1)]
-            upper = factors[0] * work[0, pl.ds(0, HALF)]
-            for k in range(1, channels):
-                row = row + factors[k] * work[channels, pl.ds(k, 1)]
-                upper = upper + factors[k] * work[k, pl.ds(0, HALF)]
-            bound[kind, v, j] = unpack(upper.astype(BF16), row, bits)
-            return 0
-
-        lax.fori_loop(0, channels, blend, 0)
+        lax.fori_loop(0, channels // 4, several, 0)
+        for v in range(channels // 4 * 4, channels):
+            grown(v)
         store(kind, j).start()
     for kind in range(2):
         for j in range(SEC):
@@ -704,6 +733,30 @@
                 grow_copy(kind, target, j).wait_send()
     for step in (1, 3, 2):
         wave_copy(step).wait_send()
+
+
+def finish(wave_in, energy_in, left_in, right_in, wave, energy, left, right, wave_held, left_held, right_held, load_sem, store_sem):
+    channels = left_in.shape[0]
+    cuts = [channels * n // 4 for n in range(5)]
+    loads, stores = [], []
+
+    def through(source, held, target, part):
+        n = len(loads)
+        loads.append(pltpu.make_async_copy(source.at[part], held.at[part], load_sem.at[n]))
+        stores.append(pltpu.make_async_copy(held.at[part], target.at[part], store_sem.at[n]))
+
+    for lo, hi in zip(cuts[:-1], cuts[1:]):
+        through(left_in, left_held, left, pl.ds(lo, hi - lo))
+        through(right_in, right_held, right, pl.ds(lo, hi - lo))
+    through(wave_in, wave_held, wave, pl.ds(0, RUN))
+    for load in loads:
+        load.start()
+    energy[0] = energy_in[0, 0]
+    for load, store in zip(loads, stores):
+        load.wait()
+        store.start()
+    for store in stores:
+        store.wait()
 
 
 def body(
@@ -761,6 +814,7 @@
             pltpu.VMEM((SLOTS, N, N), BF16),
             pltpu.VMEM((SLOTS, N, N), BF16),
             pltpu.VMEM((TERMS, channels * HALF, 2 * N), BF16),
+            pltpu.VMEM((2, -(-channels // 2) * 16, 2 * N), F32),
             pltpu.VMEM((3, SIDE * SIDE, 8, N), F32),
             pltpu.VMEM((3, 8, N), F32),
             dma((2,)),
@@ -788,7 +842,27 @@
         right_boundary[0],
         psi_start[0],
     )
-    return wave[None], energy[0, :1], left_grown[None], right_grown[None]
+    wave, energy, left_grown, right_grown = pl.pallas_call(
+        finish,
+        out_shape=(
+            jax.ShapeDtypeStruct(wave.shape, BF16),
+            jax.ShapeDtypeStruct((1,), F32),
+            jax.ShapeDtypeStruct(env, BF16),
+            jax.ShapeDtypeStruct(env, BF16),
+        ),
+        in_specs=[hbm, vmem, hbm, hbm],
+        out_specs=(hbm, smem, hbm, hbm),
+        scratch_shapes=[
+            pltpu.VMEM(wave.shape, BF16),
+            pltpu.VMEM(env, BF16),
+            pltpu.VMEM(env, BF16),
+            dma((9,)),
+            dma((9,)),
+        ],
+        compiler_params=pltpu.CompilerParams(vmem_limit_bytes=62 * 2**20),
+        name="finish",
+    )(wave, energy, left_grown, right_grown)
+    return wave[None], energy, left_grown[None], right_grown[None]
 
 
 def solution(mesh):

time: 182 us -> 174 us (0.956)
  local copies, waits for them, and re-layouts: 8.04 us -> 0 us
    unnamed x5 -> x0, local copies, waits for them, and re-layouts: 6.86 us -> none
    pallas_call x1, Pallas kernels: 170 us -> 163 us  [body(): pl.pallas_call(lambda *refs: kernel(channels, *refs), out_shape=(jax.Shap...]
    pallas_call x0 -> x1, Pallas kernels: none -> 5.99 us  [body(): pl.pallas_call(finish, out_shape=(jax.ShapeDtypeStruct(wave.shape, BF16),...]
where the time goes in v4:
time: 174 us
  Pallas kernels  173 us (99%)
    pallas_call x1, Pallas kernels, body(): pl.pallas_call(lambda *refs: kernel(channels, *refs), out_shape=(jax.Shap...  163 us
    pallas_call x1, Pallas kernels, body(): pl.pallas_call(finish, out_shape=(jax.ShapeDtypeStruct(wave.shape, BF16),...  5.99 us
    pallas_call x1, Pallas kernels, body(): pl.pallas_call(router, out_shape=jax.ShapeDtypeStruct((TABLE,), jnp.int32...  3.78 us

profile of v4, /device:TPU:64, one launch (start us, length us, event | category | flops | bytes accessed | tf_op | source)
XLA Modules:
  0.0 174.1 jit_solution(16419094142228736153)
XLA Ops:
  0.6 3.8 %router.1.refs_0_ = s32[512]{0:T(512)} custom-call(s32[1,384]{1,0:T(1,128)} %left_local.1, s32[1,384]{1,0:T(1,128)} %bitcast.10, s32[1,384]{1,0:T(1,128)} %right_local.1, s32[1,64]{1,0:T(1,128)} %left_dims.1, s32[1,64]{1,0:T(1,128)} %right_dims.1), custom_call_target="tpu_custom_call" | custom-call | tf_op jit(solution)/shard_map/router/pallas_call | solution.py:778
  4.4 163.5 %davidson.1 = (bf16[24,128,128]{2,1,0:T(8,128)(2,1)}, f32[8,128]{1,0:T(8,128)}, bf16[17,4,128,128]{3,2,1,0:T(8,128)(2,1)}, bf16[17,4,128,128]{3,2,1,0:T(8,128)(2,1)}) custom-call(s32[512]{0:T(512)} %router.1.refs_0_, f32[17,17]{1,0:T(8,128)} %refs_1_.1, f32[17,17]{1,0:T(8,128)} %refs_2_.1, bf16[17,4,128,128]{3,2,1,0:T(8,128)(2,1)} %bitcast.7, ...), custom_call_target="tpu_custom_call" | custom-call | tf_op jit(solution)/shard_map/davidson/pallas_call | solution.py:795
  167.9 6.0 %finish.1 = (bf16[24,128,128]{2,1,0:T(8,128)(2,1)}, f32[1]{0:T(128)}, bf16[17,4,128,128]{3,2,1,0:T(8,128)(2,1)}, bf16[17,4,128,128]{3,2,1,0:T(8,128)(2,1)}) custom-call(bf16[24,128,128]{2,1,0:T(8,128)(2,1)} %get-tuple-element.12.wave_in, f32[8,128]{1,0:T(8,128)} %get-tuple-element.13.energy_in, bf16[17,4,128,128]{3,2,1,0:T(8,128)(2,1)} %get-tuple-element.14.left_in, ...), custom_call_target="tpu_custom_call" | custom-call | tf_op jit(solution)/shard_map/finish/pallas_call | solution.py:845

commit v5 on v4

--- a/solution.py
+++ b/solution.py
@@ -22,6 +22,7 @@
 PACK = SEC * HALF + 16
 UNROLL = 4
 TERMS = 4
+PARTS = SLOTS // UNROLL
 RING, HAND, OPEN = 3, 7, 10
 
 SEND, SLOT_OF, LSEC, RSEC, LDIM, RDIM = 0, 32, 64, 96, 128, 160
@@ -125,11 +126,16 @@
     low = jnp.logical_and(col >= HALF, row > col - HALF)
     high = jnp.logical_and(col >= HALF, row < col - HALF)
     diag = row == col - HALF
-    return below, left, low, high, diag
+    return below, left, low, high, diag, row == col
+
+
+def triangle_bits(masks):
+    below, left, low, high, diag = [jnp.where(m, 1.0, 0.0).astype(BF16) for m in masks[:5]]
+    return below, jnp.where(masks[0], 0.0, 1.0).astype(BF16), left, low, high, diag
 
 
 def pack(block, masks):
-    below, _, _, _, diag = masks
+    below, diag = masks[0], masks[4]
     corner = block[HALF:]
     upper = jnp.where(below, pltpu.roll(corner, HALF, 1), block[:HALF])
     row = jnp.sum(jnp.where(diag, corner, 0.0), axis=0, keepdims=True)
@@ -250,10 +256,8 @@
         psi_copy(step).start()
 
     masks = triangle_masks()
-    below, left, low, high, diag = masks
-    diag_low = lax.broadcasted_iota(jnp.int32, (HALF, N), 0) == lax.broadcasted_iota(jnp.int32, (HALF, N), 1)
-    ones = [jnp.where(m, 1.0, 0.0).astype(BF16) for m in (below, left, low, high, diag)]
-    bits = (ones[0], jnp.where(below, 0.0, 1.0).astype(BF16), ones[1], ones[2], ones[3], ones[4])
+    below, diag_low = masks[0], masks[5]
+    bits = triangle_bits(masks)
     row32 = lax.broadcasted_iota(jnp.int32, (32, N), 0)
     row16 = lax.broadcasted_iota(jnp.int32, (16, N), 0)
     eye_packed = jnp.where(
@@ -339,6 +343,15 @@
             inner.append(jnp.concatenate([z[:, k * N : (k + 1) * N] for k in range(hi - lo)], axis=0))
         return [dot(beside(0, table[LSEC + s], lo, hi), z) for s, z in zip(slots, inner)]
 
+    bounds = list(range(0, channels, 5)) + [channels]
+    groups = list(zip(bounds[:-1], bounds[1:]))
+
+    def apply(lo, hi, i):
+        slots = [i * UNROLL + u for u in range(UNROLL)]
+        images = product([vec[s] for s in slots], slots, lo, hi)
+        for s, image in zip(slots, images):
+            work[HX + s] = image if lo == 0 else work[HX + s] + image
+
     def gather_step(t, _):
         @pl.when(t < channels)
         def _():
@@ -400,23 +413,25 @@
 
             lax.fori_loop(0, SIDE, open_group, 0)
 
-            bounds = list(range(0, channels, 5)) + [channels]
-            for lo, hi in zip(bounds[:-1], bounds[1:]):
-
-                @pl.when(k == hi - 1)
+            for lo, hi in groups[:-1]:
+
+                @pl.when(jnp.logical_and(k >= hi, k < hi + PARTS // 2))
                 def _():
-                    def apply(i, _):
-                        slots = [i * UNROLL + u for u in range(UNROLL)]
-                        images = product([vec[s] for s in slots], slots, lo, hi)
-                        for s, image in zip(slots, images):
-                            work[HX + s] = image if lo == 0 else work[HX + s] + image
-                        return 0
-
-                    lax.fori_loop(0, SLOTS // UNROLL, apply, 0)
+                    for n in range(2):
+                        apply(lo, hi, (k - hi) * 2 + n)
 
         return 0
 
     lax.fori_loop(0, channels + OPEN, gather_step, 0)
+    for lo, hi in groups:
+        done = min(max(channels - hi, 0) * 2, PARTS) if hi < channels else 0
+
+        def rest(i, _):
+            apply(lo, hi, i)
+            return 0
+
+        if done < PARTS:
+            lax.fori_loop(done, PARTS, rest, 0)
 
     for step in (1, 3, 2):
         psi_copy(step).wait_send()
@@ -448,18 +463,12 @@
                 device_id_type=MESH,
             )
 
-        def begin(d, _):
+        for d in range(1, SIDE * SIDE):
             copy(d).start()
-            return 0
-
-        lax.fori_loop(1, SIDE * SIDE, begin, 0)
         red[number, me] = mine[number]
 
-        def end(d, _):
+        for d in range(1, SIDE * SIDE):
             copy(d).wait()
-            return 0
-
-        lax.fori_loop(1, SIDE * SIDE, end, 0)
         total = jnp.sum(red[number], axis=0)
         total = jnp.broadcast_to(jnp.sum(total, axis=1, keepdims=True), (8, N))
         return [total[i : i + 1] for i in range(len(parts))]
@@ -678,7 +687,7 @@
 
     def store(kind, j):
         out = left_out if kind == 0 else right_out
-        return pltpu.make_async_copy(bound.at[kind, :, j], out.at[:, j], store_sem.at[kind, j])
+        return pltpu.make_async_copy(bound.at[kind, :, j, pl.ds(0, HALF + 16)], out.at[:, j], store_sem.at[kind, j])
 
     for j, kind in [(j, kind) for j in (0, 2, 1, 3) for kind in range(2)]:
         for target in (1, 2):
@@ -713,18 +722,10 @@
                 for n in range(count):
                     work[32 + v, pl.ds((start + n) * 8, 8)] = mixed[v * 8 : v * 8 + 8, n * N : n * N + N]
 
-        def grown(v):
-            upper = work[32 + v, pl.ds(0, HALF)].astype(BF16)
-            bound[kind, v, j] = unpack(upper, work[32 + v, pl.ds(HALF, 1)], bits)
-
-        def several(i, _):
-            for n in range(4):
-                grown(i * 4 + n)
-            return 0
-
-        lax.fori_loop(0, channels // 4, several, 0)
-        for v in range(channels // 4 * 4, channels):
-            grown(v)
+        for v in range(channels):
+            row = jnp.broadcast_to(work[32 + v, pl.ds(HALF, 1)], (16, N))
+            bound[kind, v, j, pl.ds(0, HALF)] = work[32 + v, pl.ds(0, HALF)].astype(BF16)
+            bound[kind, v, j, pl.ds(HALF, 16)] = row.astype(BF16)
         store(kind, j).start()
     for kind in range(2):
         for j in range(SEC):
@@ -735,28 +736,46 @@
         wave_copy(step).wait_send()
 
 
-def finish(wave_in, energy_in, left_in, right_in, wave, energy, left, right, wave_held, left_held, right_held, load_sem, store_sem):
+def finish(wave_in, energy_in, left_in, right_in, wave, energy, left, right, wave_held, packed, whole, load_sem, store_sem):
     channels = left_in.shape[0]
-    cuts = [channels * n // 4 for n in range(5)]
-    loads, stores = [], []
-
-    def through(source, held, target, part):
-        n = len(loads)
-        loads.append(pltpu.make_async_copy(source.at[part], held.at[part], load_sem.at[n]))
-        stores.append(pltpu.make_async_copy(held.at[part], target.at[part], store_sem.at[n]))
-
-    for lo, hi in zip(cuts[:-1], cuts[1:]):
-        through(left_in, left_held, left, pl.ds(lo, hi - lo))
-        through(right_in, right_held, right, pl.ds(lo, hi - lo))
-    through(wave_in, wave_held, wave, pl.ds(0, RUN))
-    for load in loads:
-        load.start()
+    cuts = [channels * n // 6 for n in range(7)]
+    parts = [(kind, lo, hi) for lo, hi in zip(cuts[:-1], cuts[1:]) for kind in range(2)]
+
+    def load(n):
+        kind, lo, hi = parts[n]
+        source = (left_in, right_in)[kind]
+        return pltpu.make_async_copy(
+            source.at[pl.ds(lo, hi - lo)], packed.at[kind, pl.ds(lo, hi - lo)], load_sem.at[n]
+        )
+
+    def store(n):
+        kind, lo, hi = parts[n]
+        target = (left, right)[kind]
+        return pltpu.make_async_copy(
+            whole.at[kind, pl.ds(lo, hi - lo)], target.at[pl.ds(lo, hi - lo)], store_sem.at[n]
+        )
+
+    wave_load = pltpu.make_async_copy(wave_in, wave_held, load_sem.at[len(parts)])
+    wave_store = pltpu.make_async_copy(wave_held, wave, store_sem.at[len(parts)])
+    for n in range(len(parts)):
+        load(n).start()
+        if n == 1:
+            wave_load.start()
     energy[0] = energy_in[0, 0]
-    for load, store in zip(loads, stores):
-        load.wait()
-        store.start()
-    for store in stores:
-        store.wait()
+    bits = triangle_bits(triangle_masks())
+    for n, (kind, lo, hi) in enumerate(parts):
+        load(n).wait()
+
+        for k, j in [(k, j) for k in range(lo, hi) for j in range(SEC)]:
+            row = packed[kind, k, j, pl.ds(HALF, 16)].astype(F32)[:1]
+            whole[kind, k, j] = unpack(packed[kind, k, j, pl.ds(0, HALF)], row, bits)
+        store(n).start()
+        if n == 1:
+            wave_load.wait()
+            wave_store.start()
+    for n in range(len(parts)):
+        store(n).wait()
+    wave_store.wait()
 
 
 def body(
@@ -797,8 +816,8 @@
         out_shape=(
             jax.ShapeDtypeStruct((RUN, N, N), BF16),
             jax.ShapeDtypeStruct((8, N), F32),
-            jax.ShapeDtypeStruct(env, BF16),
-            jax.ShapeDtypeStruct(env, BF16),
+            jax.ShapeDtypeStruct((channels, SEC, HALF + 16, N), BF16),
+            jax.ShapeDtypeStruct((channels, SEC, HALF + 16, N), BF16),
         ),
         in_specs=[smem, smem, smem, hbm, hbm, vmem],
         out_specs=(vmem, vmem, hbm, hbm),
@@ -854,10 +873,10 @@
         out_specs=(hbm, smem, hbm, hbm),
         scratch_shapes=[
             pltpu.VMEM(wave.shape, BF16),
-            pltpu.VMEM(env, BF16),
-            pltpu.VMEM(env, BF16),
-            dma((9,)),
-            dma((9,)),
+            pltpu.VMEM((2, channels, SEC, HALF + 16, N), BF16),
+            pltpu.VMEM((2,) + env, BF16),
+            dma((13,)),
+            dma((13,)),
         ],
         compiler_params=pltpu.CompilerParams(vmem_limit_bytes=62 * 2**20),
         name="finish",

time: 174 us -> 170 us (0.977)
  Pallas kernels: 173 us -> 169 us
    pallas_call x1, Pallas kernels: 163 us -> 159 us  [body(): pl.pallas_call(lambda *refs: kernel(channels, *refs), out_shape=(jax.Shap...]
where the time goes in v5:
time: 170 us; the launch traced here: 169 us
  Pallas kernels  169 us (99%)
    pallas_call x1, Pallas kernels, body(): pl.pallas_call(lambda *refs: kernel(channels, *refs), out_shape=(jax.Shap...  159 us
    pallas_call x1, Pallas kernels, body(): pl.pallas_call(finish, out_shape=(jax.ShapeDtypeStruct(wave.shape, BF16),...  5.94 us
    pallas_call x1, Pallas kernels, body(): pl.pallas_call(router, out_shape=jax.ShapeDtypeStruct((TABLE,), jnp.int32...  3.78 us

profile of v5, /device:TPU:64, one launch (start us, length us, event | category | flops | bytes accessed | tf_op | source)
XLA Modules:
  0.0 169.4 jit_solution(10320174477367386274)
XLA Ops:
  0.6 3.8 %router.1.refs_0_ = s32[512]{0:T(512)} custom-call(s32[1,384]{1,0:T(1,128)} %left_local.1, s32[1,384]{1,0:T(1,128)} %bitcast.10, s32[1,384]{1,0:T(1,128)} %right_local.1, s32[1,64]{1,0:T(1,128)} %left_dims.1, s32[1,64]{1,0:T(1,128)} %right_dims.1), custom_call_target="tpu_custom_call" | custom-call | tf_op jit(solution)/shard_map/router/pallas_call | solution.py:797
  4.4 158.8 %davidson.1 = (bf16[24,128,128]{2,1,0:T(8,128)(2,1)}, f32[8,128]{1,0:T(8,128)}, bf16[17,4,80,128]{3,2,1,0:T(8,128)(2,1)}, bf16[17,4,80,128]{3,2,1,0:T(8,128)(2,1)}) custom-call(s32[512]{0:T(512)} %router.1.refs_0_, f32[17,17]{1,0:T(8,128)} %refs_1_.1, f32[17,17]{1,0:T(8,128)} %refs_2_.1, bf16[17,4,128,128]{3,2,1,0:T(8,128)(2,1)} %bitcast.7, ...), custom_call_target="tpu_custom_call" | custom-call | tf_op jit(solution)/shard_map/davidson/pallas_call | solution.py:814
  163.3 5.9 %finish.1 = (bf16[24,128,128]{2,1,0:T(8,128)(2,1)}, f32[1]{0:T(128)}, bf16[17,4,128,128]{3,2,1,0:T(8,128)(2,1)}, bf16[17,4,128,128]{3,2,1,0:T(8,128)(2,1)}) custom-call(bf16[24,128,128]{2,1,0:T(8,128)(2,1)} %get-tuple-element.12.wave_in, f32[8,128]{1,0:T(8,128)} %get-tuple-element.13.energy_in, bf16[17,4,80,128]{3,2,1,0:T(8,128)(2,1)} %get-tuple-element.14.left_in, ...), custom_call_target="tpu_custom_call" | custom-call | tf_op jit(solution)/shard_map/finish/pallas_call | solution.py:864

commit v6 on v5

--- a/solution.py
+++ b/solution.py
@@ -482,7 +482,12 @@
         work[HX + s] = image
         return ss + fold(start * start), sh + fold(start * image), hh + fold(image * image)
 
-    ss, sh, hh = exchange(0, lax.fori_loop(0, SLOTS, first_sums, (zero8,) * 3))
+    def several_sums(i, sums):
+        for u in range(UNROLL):
+            sums = first_sums(i * UNROLL + u, sums)
+        return sums
+
+    ss, sh, hh = exchange(0, lax.fori_loop(0, SLOTS // UNROLL, several_sums, (zero8,) * 3))
     norm = jnp.sqrt(ss)
     xx = ss / (norm * norm)
     a = sh / (norm * norm)
@@ -556,7 +561,12 @@
         vectr[s] = pltpu.roll(turned.astype(F32), HALF, 1).astype(BF16)
         return 0
 
-    lax.fori_loop(0, SLOTS, final_vector, 0)
+    def final_vectors(i, _):
+        for u in range(UNROLL):
+            final_vector(i * UNROLL + u, 0)
+        return 0
+
+    lax.fori_loop(0, SLOTS // UNROLL, final_vectors, 0)
 
     def wave_copy(step):
         to_w = (my_w + step) % SIDE
@@ -655,19 +665,20 @@
         grow(kind, my_group(kind, SIDE - 1), 2)
         for j in (0, 1):
             grow_copy(kind, 2, j).start()
+    rows = 160 if deep % 160 == 0 else 32
     for j in (0, 2, 1, 3):
         target = 1 if j < 2 else 2
         for kind in range(2):
             grow_copy(kind, 0, j).wait_recv()
 
             def add(i, _):
-                there = pl.ds(pl.multiple_of(target * region + j * deep + i * 32, 16), 32)
-                here = pl.ds(pl.multiple_of(j * deep + i * 32, 16), 32)
+                there = pl.ds(pl.multiple_of(target * region + j * deep + i * rows, 16), rows)
+                here = pl.ds(pl.multiple_of(j * deep + i * rows, 16), rows)
                 total = outb[kind, there].astype(F32) + gath[kind, here].astype(F32)
                 outb[kind, there] = total.astype(BF16)
                 return 0
 
-            lax.fori_loop(0, deep // 32, add, 0)
+            lax.fori_loop(0, deep // rows, add, 0)
             grow_copy(kind, target, j).start()
     for kind in range(2):
         grow(kind, my_group(kind, 0), 3)

time: 170 us -> 167 us (0.982)
  Pallas kernels: 169 us -> 165 us
    pallas_call x1, Pallas kernels: 159 us -> 156 us  [body(): pl.pallas_call(lambda *refs: kernel(channels, *refs), out_shape=(jax.Shap...]
where the time goes in v6:
time: 167 us; the launch traced here: 166 us
  Pallas kernels  165 us (99%)
    pallas_call x1, Pallas kernels, body(): pl.pallas_call(lambda *refs: kernel(channels, *refs), out_shape=(jax.Shap...  156 us
    pallas_call x1, Pallas kernels, body(): pl.pallas_call(finish, out_shape=(jax.ShapeDtypeStruct(wave.shape, BF16),...  5.94 us
    pallas_call x1, Pallas kernels, body(): pl.pallas_call(router, out_shape=jax.ShapeDtypeStruct((TABLE,), jnp.int32...  3.78 us

profile of v6, /device:TPU:64, one launch (start us, length us, event | category | flops | bytes accessed | tf_op | source)
XLA Modules:
  0.0 166.2 jit_solution(3587433908824924404)
XLA Ops:
  0.6 3.8 %router.1.refs_0_ = s32[512]{0:T(512)} custom-call(s32[1,384]{1,0:T(1,128)} %left_local.1, s32[1,384]{1,0:T(1,128)} %bitcast.10, s32[1,384]{1,0:T(1,128)} %right_local.1, s32[1,64]{1,0:T(1,128)} %left_dims.1, s32[1,64]{1,0:T(1,128)} %right_dims.1), custom_call_target="tpu_custom_call" | custom-call | tf_op jit(solution)/shard_map/router/pallas_call | solution.py:808
  4.4 155.6 %davidson.1 = (bf16[24,128,128]{2,1,0:T(8,128)(2,1)}, f32[8,128]{1,0:T(8,128)}, bf16[17,4,80,128]{3,2,1,0:T(8,128)(2,1)}, bf16[17,4,80,128]{3,2,1,0:T(8,128)(2,1)}) custom-call(s32[512]{0:T(512)} %router.1.refs_0_, f32[17,17]{1,0:T(8,128)} %refs_1_.1, f32[17,17]{1,0:T(8,128)} %refs_2_.1, bf16[17,4,128,128]{3,2,1,0:T(8,128)(2,1)} %bitcast.7, ...), custom_call_target="tpu_custom_call" | custom-call | tf_op jit(solution)/shard_map/davidson/pallas_call | solution.py:825
  160.0 5.9 %finish.1 = (bf16[24,128,128]{2,1,0:T(8,128)(2,1)}, f32[1]{0:T(128)}, bf16[17,4,128,128]{3,2,1,0:T(8,128)(2,1)}, bf16[17,4,128,128]{3,2,1,0:T(8,128)(2,1)}) custom-call(bf16[24,128,128]{2,1,0:T(8,128)(2,1)} %get-tuple-element.12.wave_in, f32[8,128]{1,0:T(8,128)} %get-tuple-element.13.energy_in, bf16[17,4,80,128]{3,2,1,0:T(8,128)(2,1)} %get-tuple-element.14.left_in, ...), custom_call_target="tpu_custom_call" | custom-call | tf_op jit(solution)/shard_map/finish/pallas_call | solution.py:875
